TPU v7x, 128 devices: a whole 4x4x4 slice. The times are simulated.
128 devices in a mesh: row: 8 (over z, y_lo), col: 16 (over y_hi, x, core).
Axes of the slice: x: 4, y: 4 (y_hi: 2, y_lo: 2; y = y_hi * 2 + y_lo), z: 4, core: 2. Of those that a mesh axis runs over, the one named last changes fastest.
Arguments:
- points: float32 [4, 4, 1048576], P(None, None, ('row', 'col')), may hold values from -0.4 to 1.4, as said below
- density: float32 [1048576], P(('row', 'col')), may hold values from -6 to 6
- near_pairs: int32 [768, 2], P(('row', 'col')), may hold values from 0 to 255, as said below
- far_pairs: int32 [2048, 2], P(('row', 'col')), may hold values from 0 to 255, as said below
- near_count: int32 [128], P(('row', 'col')), may hold values from 1 to 6
- far_count: int32 [128], P(('row', 'col')), may hold values from 1 to 16
Outputs:
- potential: float32 [1048576], P(('row', 'col'))
Inputs may be any that keep to these rules, and one draw needn't show every extreme that they name: `near_pairs`: the first column indexes target band blocks and the second source band blocks (below 128). On device (r, c) the first column lies in c * 16 to c * 16 + 15, so every near target block is one of the device's own blocks. The first slot of each device names one of its own blocks k as (c * 16 + k, r * 16 + k). `far_pairs`: the first column indexes target band blocks (below 256), the second source band blocks (below 128). `points`: weights (entry 3) lie in 0.01 to 0.04; coordinates in -0.4 to 1.4.
All inputs are finite; a program needn't handle non-finite values.
Results may differ from a plain program's by a relative error of at most 0.0003.
Values sent between devices are 32-bit elements; how exact they have to be, the bound alone decides.
A program may use at most 64 MiB of HBM per device.

v0:
```python
import jax
import jax.numpy as jnp
from jax import lax
from jax.sharding import PartitionSpec as P

BLK = 512


soft_sq = 0.0004


def centroids(blocked):
    weight = jnp.sum(blocked[3], axis=0)
    place = jnp.sum(blocked[:3] * blocked[3][None], axis=1) / weight[None]
    return jnp.concatenate([place, weight[None]], axis=0)


def far_tile(left, right):
    dist = jnp.zeros((left.shape[1], right.shape[1]), jnp.float32)
    for k in range(3):
        diff = left[k][:, None] - right[k][None, :]
        dist = dist + diff * diff
    return left[3][:, None] * right[3][None, :] * lax.rsqrt(dist + soft_sq)


def near_tile(left, right):
    total = jnp.zeros((left.shape[2], right.shape[2]), jnp.float32)
    for u in range(left.shape[1]):
        for v in range(right.shape[1]):
            dist = jnp.zeros((left.shape[2], right.shape[2]), jnp.float32)
            for k in range(3):
                diff = left[k, u][:, None] - right[k, v][None, :]
                dist = dist + diff * diff
            total = total + left[3, u][:, None] * right[3, v][None, :] * lax.rsqrt(dist + soft_sq)
    return total


def body(points, density, near_pairs, far_pairs, near_count, far_count):
    quad = points.shape[1]
    per_dev = points.shape[2] // BLK
    own_blocks = points.reshape(4, quad, per_dev, BLK)
    row_pts, row_flat = (
        lax.all_gather(points, "col", axis=2, tiled=True),
        lax.all_gather(density, "col", axis=0, tiled=True),
    )
    row_cent = centroids(row_pts.reshape(4, quad, -1, BLK))
    col_pts, col_flat = (
        lax.all_gather(points, "row", axis=2, tiled=True),
        lax.all_gather(density, "row", axis=0, tiled=True),
    )
    col_blocks = col_pts.reshape(4, quad, -1, BLK)
    row_dens = row_flat.reshape(-1, BLK)
    col_dens = col_flat.reshape(-1, BLK)
    col_cent = centroids(col_blocks)
    row_idx = lax.axis_index("row")
    col_idx = lax.axis_index("col")

    def accumulate(acc, tile, a, b):
        row_acc, col_acc = acc
        same = (row_idx == b // per_dev) & (col_idx == a // per_dev) & (a % per_dev == b % per_dev)
        mirror = jnp.where(same, 0.0, 1.0).astype(jnp.float32)
        dens_a = lax.dynamic_index_in_dim(row_dens, a, 0, keepdims=False)
        dens_b = lax.dynamic_index_in_dim(col_dens, b, 0, keepdims=False)
        to_rows = jnp.dot(tile, dens_b, precision=lax.Precision.HIGHEST)
        to_cols = mirror * jnp.dot(dens_a, tile, precision=lax.Precision.HIGHEST)
        return (row_acc.at[a].add(to_rows), col_acc.at[b].add(to_cols))

    def near_step(slot, acc):
        a = near_pairs[slot, 0]
        b = near_pairs[slot, 1]
        local = a - col_idx * per_dev
        left = lax.dynamic_index_in_dim(own_blocks, local, 2, keepdims=False)
        right = lax.dynamic_index_in_dim(col_blocks, b, 2, keepdims=False)
        return accumulate(acc, near_tile(left, right), a, b)

    def far_step(slot, acc):
        a = far_pairs[slot, 0]
        b = far_pairs[slot, 1]
        left = lax.dynamic_index_in_dim(row_cent, a, 1, keepdims=False)
        right = lax.dynamic_index_in_dim(col_cent, b, 1, keepdims=False)
        return accumulate(acc, far_tile(left, right), a, b)

    start = (jnp.zeros(row_dens.shape, jnp.float32), jnp.zeros(col_dens.shape, jnp.float32))
    acc = lax.fori_loop(0, near_count[0], near_step, start)
    row_acc, col_acc = lax.fori_loop(0, far_count[0], far_step, acc)
    from_rows = lax.psum_scatter(row_acc.reshape(-1), "col", scatter_dimension=0, tiled=True)
    from_cols = lax.psum_scatter(col_acc.reshape(-1), "row", scatter_dimension=0, tiled=True)
    return from_rows + from_cols


def solution(mesh):
    in_specs = (
        P(None, None, ("row", "col")),
        P(("row", "col")),
        P(("row", "col"), None),
        P(("row", "col"), None),
        P(("row", "col")),
        P(("row", "col")),
    )
    out_specs = P(("row", "col"))
    return jax.shard_map(body, mesh=mesh, in_specs=in_specs, out_specs=out_specs, check_vma=False)
```

profile of v0, /device:TPU:0, one launch (start us, length us, event | category | flops | bytes accessed | tf_op | source)
XLA Modules:
  0.0 733.8 jit_solution(7891615701411540431)
XLA Ops:
  8.1 1.4 reshape.233
  9.5 26.1 %all_gather.14 = f32[131072]{0:T(1024)S(1)} all-gather(f32[8192]{0:T(1024)S(1)} %copy-done.4), channel_id=1, replica_groups=mesh['row'=8,'col'=16] {'col'}, dimensions={0}, use_global_device_ids=true | all-gather | bytes 557056 | tf_op jit(solution)/shard_map/all_gather | solution.py:44
  35.7 31.5 %all_gather.13 = f32[65536]{0:T(1024)S(1)} all-gather(f32[8192]{0:T(1024)S(1)} %copy-done.4), channel_id=1, replica_groups=mesh['row'=8,'col'=16] {'row'}, dimensions={0}, use_global_device_ids=true | all-gather | bytes 294912 | tf_op jit(solution)/shard_map/all_gather | solution.py:49
  67.3 42.1 %all-gather.3.cloned.1.call-done = f32[4,4,65536]{2,1,0:T(4,128)} async-done(((f32[4,4,8192]{2,1,0:T(4,128)}), f32[4,4,65536]{2,1,0:T(4,128)}) %all-gather.3.cloned.1.call-update) | async-done | bytes 4194320 | tf_op jit(solution)/shard_map/all_gather | solution.py:48
  109.3 2.0 slice_bitcast_fusion.1
  111.4 6.1 reshape.234
  117.5 4.3 fusion.35
  122.0 1.1 pad_maximum_fusion.1
  123.3 44.7 %while.34 = (s32[]{:T(128)}, f32[256,512]{1,0:T(8,128)S(1)}, f32[128,512]{1,0:T(8,128)S(1)}, s32[]{:T(128)}, s32[6,2]{0,1:T(2,128)S(1)}, /*index=5*/s32[]{:T(128...) while((s32[]{:T(128)}, f32[256,512]{1,0:T(8,128)S(1)}, ...), condition=%wide.region_3.0_spmd, body=%wide.region_0.3_spmd.sunk | while | flops 56363552 | bytes 3634019 | solution.py:84
  127.2 1.0 constant_dynamic-slice_fusion.23
  128.3 7.8 %multiply_add_fusion.2 = f32[512,512]{1,0:T(8,128)S(1)} fusion(f32[512]{0:T(512)S(1)} %bitcast.228, f32[512]{0:T(512)S(1)} %bitcast.229, f32[512]{0:T(512)S(1)} %bitcast.230, f32[512]{0:T(512)S(1)} %bitcast.231, f32[512]{0:T(512)S(1)} %bitcast.232, f32[512]{0:T(512)S(1)} %bitcast.233, f32[512]{0:T(512)S(1)} %bitcast.234, f32[512]{0:T(512)S(1)} %bitcast.235, ...), kind=kLoop, calls=%fused_computation.2.clone.1 | loop fusion | flops 50069504 | bytes 1114112 | tf_op jit(solution)/shard_map/while/body/add | solution.py:34
  143.6 1.6 fusion.58
  149.0 1.0 constant_dynamic-slice_fusion.23
  150.1 7.8 %multiply_add_fusion.2 = f32[512,512]{1,0:T(8,128)S(1)} fusion(f32[512]{0:T(512)S(1)} %bitcast.228, f32[512]{0:T(512)S(1)} %bitcast.229, f32[512]{0:T(512)S(1)} %bitcast.230, f32[512]{0:T(512)S(1)} %bitcast.231, f32[512]{0:T(512)S(1)} %bitcast.232, f32[512]{0:T(512)S(1)} %bitcast.233, f32[512]{0:T(512)S(1)} %bitcast.234, f32[512]{0:T(512)S(1)} %bitcast.235, ...), kind=kLoop, calls=%fused_computation.2.clone.1 | loop fusion | flops 50069504 | bytes 1114112 | tf_op jit(solution)/shard_map/while/body/add | solution.py:34
  165.4 1.6 fusion.58
  168.0 0.8 copy-done.2
  169.5 13.7 %all-gather.5.cloned.1.call-done = f32[4,4,131072]{2,1,0:T(4,128)} async-done(((f32[4,4,8192]{2,1,0:T(4,128)}), f32[4,4,131072]{2,1,0:T(4,128)}) %all-gather.5.cloned.1.call-update) | async-done | bytes 8388624 | tf_op jit(solution)/shard_map/all_gather | solution.py:43
  183.1 3.1 slice_bitcast_fusion
  186.2 0.9 div.49
  187.1 0.9 broadcast_in_dim.20
  188.0 7.5 %fusion.34 = f32[3,131072]{1,0:T(4,128)S(1)} fusion(f32[4,4,131072]{2,1,0:T(4,128)} %all-gather.5.cloned.1.call-done, f32[4,131072]{1,0:T(4,128)S(1)} %get-tuple-element.523), kind=kLoop, calls=%fused_computation.69 | loop fusion | flops 2752512 | bytes 9961472 | tf_op jit(solution)/shard_map/reduce_sum | solution.py:14
  197.3 49.6 %while.35 = (s32[]{:T(128)}, f32[256,512]{1,0:T(8,128)S(1)}, f32[128,512]{1,0:T(8,128)S(1)}, s32[]{:T(128)}, s32[16,2]{0,1:T(2,128)S(1)}, /*index=5*/f32[4,256,5...) while((s32[]{:T(128)}, f32[256,512]{1,0:T(8,128)S(1)}, ...), condition=%wide.region_11.12_spmd, body=%wide.region_8.11_spmd.sunk | while | flops 12061258 | bytes 97120 | solution.py:85
  207.4 1.8 fusion.63
  210.6 2.9 fusion.62
  223.7 1.8 fusion.63
  227.0 2.9 fusion.62
  240.0 1.8 fusion.63
  243.3 2.9 fusion.62
  247.7 0.9 copy.11
  251.1 334.5 %all-reduce.7.cloned.1.call-done = f32[65536]{0:T(1024)} async-done(((f32[65536]{0:T(1024)}), f32[65536]{0:T(1024)}) %all-reduce.7.cloned.1.call-update) | async-done | bytes 262160
  585.7 140.2 %all-reduce.5.cloned.1.call-done = f32[131072]{0:T(1024)} async-done(((f32[131072]{0:T(1024)}), f32[131072]{0:T(1024)}) %all-reduce.5.cloned.1.call-update) | async-done | bytes 524304
  725.9 1.4 dynamic-slice_add_fusion
  (84 shorter events, 20.8 us)
Async XLA Ops:
  6.5 2.9 copy-start.4
  6.5 102.8 %all-gather.3.cloned.1.call-start = ((), (), s32[]{:S(2)}) async-start(), calls=%async_computation | async-start | bytes 4718592 | tf_op jit(solution)/shard_map/all_gather | solution.py:48
  7.3 175.9 %all-gather.5.cloned.1.call-start = ((), (), s32[]{:S(2)}) async-start(), calls=%async_computation.1 | async-start | bytes 8912896 | tf_op jit(solution)/shard_map/all_gather | solution.py:43
  8.0 577.7 %all-reduce.7.cloned.1.call-start = ((), (), s32[]{:S(2)}) async-start(), calls=%async_computation.3 | async-start | bytes 524288
  121.7 1.5 copy-start.5
  121.8 1.5 copy-start.6
  121.8 1.5 copy-start.7
  167.9 0.8 copy-start.2
  168.8 0.7 copy-start.3
  188.0 7.5 %copy-start.1 = (f32[256,512]{1,0:T(8,128)S(1)}, f32[256,512]{1,0:T(8,128)}, u32[]{:S(2)}) copy-start(f32[256,512]{1,0:T(8,128)} %div.49) | copy-start | bytes 1572868
  195.6 1.0 copy-start
  196.6 0.7 copy-start.8
  246.9 1.8 copy-start.10
  246.9 2.4 copy-start.9
  247.7 478.2 %all-reduce.5.cloned.1.call-start = ((), (), s32[]{:S(2)}) async-start(), calls=%async_computation.2 | async-start | bytes 1048576
Sparse Core Ops, SparseCore 0:
  9.0 100.2 all-gather.2
  111.8 71.2 all-gather.4
  247.8 337.8 all-reduce.6
  588.2 137.6 all-reduce.4
where the time goes:
time: 742 us; the launch traced here: 734 us
  waiting for transfers between devices  532 us (72%)
  blocking collectives  57.7 us (8%)
  loops' own time  45 us (6%)
  other arithmetic  42.7 us (6%)
  local copies, waits for them, and re-layouts  23.3 us (3%)
  matrix products  18.5 us (2%)
  between operations  14.6 us (2%)
    unnamed x6, waiting for transfers between devices  476 us
    all_gather x1, waiting for transfers between devices, body(): lax.all_gather(points, 'row', axis=2, tiled=True)  42.1 us
    all_gather x1, blocking collectives, body(): lax.all_gather(density, 'row', axis=0, tiled=True)  31.5 us
    another operation x1, loops' own time, body(): row_acc, col_acc = lax.fori_loop(0, far_count[0], far_step, acc)  26.7 us
    all_gather x1, blocking collectives, body(): lax.all_gather(density, 'col', axis=0, tiled=True)  26.1 us
    another operation x1, loops' own time, body(): acc = lax.fori_loop(0, near_count[0], near_step, start)  18.3 us
    add x2, other arithmetic, near_tile(): total + left[3, u][:, None] * right[3, v][None, :] * lax.rsqrt(dist + sof...  15.6 us
  transfers between devices with their start and end apart: 4, of which 4 were waited for; matrix products, arithmetic and copies ran while one was open for 6% of the time, Pallas kernels for 0%

commit v1 on v0

v1 whole, which is shorter than its diff:
```python
import jax
import jax.numpy as jnp
from jax import lax
from jax.experimental import pallas as pl
from jax.experimental.pallas import tpu as pltpu
from jax.sharding import PartitionSpec as P

BLK = 512
BPD = 16
NNEAR = 6
NFAR = 16
N_ROW = 8
N_COL = 16
soft_sq = 0.0004

MESH = pl.DeviceIdType.MESH
F32 = jnp.float32
BF16 = jnp.bfloat16
NREM = NNEAR - 1
LIST = 64


def vmem(*shape, dtype=F32):
    return pltpu.VMEM(shape, dtype)


def owner_of(block):
    return lax.shift_right_logical(block, 4)


def within(block):
    return block & (BPD - 1)


def same_rows(a, b):
    return jnp.full((1, BLK), a, jnp.int32) == jnp.full((1, BLK), b, jnp.int32)


def exchange_kernel(
    pts, dens, npairs, fpairs,
    near_out, near_dens, far_i, far_j, own_dens,
    lists, stage, blocks, cent_i, cent_j, sel_i, sel_j, got_i, got_j, pack, packd, nrecv, nrecvd,
    lsend, lrecv, xsend, xrecv, zsend, zrecv, nsend, nrcv, dsend, drcv, ysend, yrecv,
):
    r = lax.axis_index("row")
    c = lax.axis_index("col")
    z, ylo = r // 2, lax.rem(r, 2)
    yhi, xc = c // 8, lax.rem(c, 8)
    x, core = xc // 2, lax.rem(xc, 2)
    row_peers = [(lax.rem(r + i, N_ROW), c) for i in range(1, N_ROW)]
    x_peers = [(r, yhi * 8 + lax.rem(x + i, 4) * 2 + core) for i in range(1, 4)]
    core_peer = (r, yhi * 8 + x * 2 + 1 - core)
    y_far = (r, lax.rem(c + 8, N_COL))
    y_near = (r + 1 - 2 * ylo, c)

    barrier = pltpu.get_barrier_semaphore()
    everyone = row_peers + x_peers + [core_peer, y_far]
    for p in everyone:
        pl.semaphore_signal(barrier, inc=1, device_id=p, device_id_type=MESH)

    for s in range(NNEAR):
        stage[s] = npairs[s, 0]
        stage[NNEAR + s] = npairs[s, 1]
    for s in range(NFAR):
        stage[16 + s] = fpairs[s, 0]
        stage[32 + s] = fpairs[s, 1]

    def centroid(k, _):
        cols = pl.ds(pl.multiple_of(k * BLK, BLK), BLK)
        blocks[k] = pts[:, :, cols]
        w = pts[3, :, cols]
        total = jnp.sum(w, axis=0, keepdims=True)
        for d in range(3):
            cent_i[xc, d, pl.ds(k, 1), :] = jnp.sum(pts[d, :, cols] * w, axis=0, keepdims=True) / total
        cent_i[xc, 3, pl.ds(k, 1), :] = total
        return 0

    lax.fori_loop(0, BPD, centroid, 0)
    for q in range(4):
        cent_i[xc, 4, :, q * 128 : (q + 1) * 128] = dens[pl.ds(q, BPD, stride=4), :]
    cent_j[z] = cent_i[xc]
    own_dens[...] = cent_i[xc, 4]

    pl.semaphore_wait(barrier, len(everyone))

    def remote(src, dst, send, recv, peer):
        copy = pltpu.make_async_remote_copy(
            src_ref=src, dst_ref=dst, send_sem=send, recv_sem=recv, device_id=peer, device_id_type=MESH
        )
        copy.start()
        return copy

    pending = []
    list_copies = [remote(stage, lists.at[r], lsend.at[i], lrecv.at[i], p) for i, p in enumerate(row_peers)]
    list_copies.append(remote(stage, lists.at[N_ROW], lsend.at[7], lrecv.at[7], y_far))
    x_copies = [remote(cent_i.at[xc], cent_i.at[xc], xsend.at[i], xrecv.at[i], p) for i, p in enumerate(x_peers)]
    x_copies.append(remote(cent_i.at[xc], cent_i.at[xc], xsend.at[3], xrecv.at[3], core_peer))
    z_copies = [
        remote(cent_j.at[z], cent_j.at[z], zsend.at[i - 1], zrecv.at[i - 1], (lax.rem(z + i, 4) * 2 + ylo, c))
        for i in range(1, 4)
    ]

    for copy in list_copies:
        copy.wait_recv()
    near_copies = []
    for i in range(N_ROW):
        peer = lax.rem(r + i, N_ROW)
        if i == 0:
            source = stage
        else:
            source = lists.at[peer]

        def fill(s, _, i=i, source=source):
            k = within(source[NNEAR + 1 + s])
            if i == 0:
                nrecv[r, s] = blocks[k]
                nrecvd[r, pl.ds(s, 1), :] = own_dens[pl.ds(k, 1), :]
            else:
                pack[i - 1, s] = blocks[k]
                packd[i - 1, pl.ds(s, 1), :] = own_dens[pl.ds(k, 1), :]
            return 0

        lax.fori_loop(0, NREM, fill, 0)
        if i > 0:
            near_copies.append(remote(pack.at[i - 1], nrecv.at[r], nsend.at[i - 1], nrcv.at[i - 1], (peer, c)))
            near_copies.append(remote(packd.at[i - 1], nrecvd.at[r], dsend.at[i - 1], drcv.at[i - 1], (peer, c)))

    relays = []
    for i in range(1, 4):
        x_copies[i - 1].wait_recv()
        g = lax.rem(x - i + 4, 4) * 2 + core
        relays.append(remote(cent_i.at[g], cent_i.at[g], xsend.at[3 + i], xrecv.at[3 + i], core_peer))
    x_copies[3].wait_recv()
    for copy in relays:
        copy.wait_recv()

    def choose_i(s, _):
        a = lists[N_ROW, 16 + s]
        g, k = owner_of(a) & 7, within(a)
        for f in range(5):
            sel_i[f, pl.ds(s, 1), :] = cent_i[g, f, pl.ds(k, 1), :]
        return 0

    lax.fori_loop(0, NFAR, choose_i, 0)
    y_copies = [remote(sel_i, got_i, ysend.at[0], yrecv.at[0], y_far)]

    for copy in z_copies:
        copy.wait_recv()
    near_row = y_near[0]

    def choose_j(s, _):
        b = lists[near_row, 32 + s]
        g, k = lax.shift_right_logical(owner_of(b), 1), within(b)
        for f in range(5):
            sel_j[f, pl.ds(s, 1), :] = cent_j[g, f, pl.ds(k, 1), :]
        return 0

    lax.fori_loop(0, NFAR, choose_j, 0)
    y_copies.append(remote(sel_j, got_j, ysend.at[1], yrecv.at[1], y_near))

    y_copies[0].wait_recv()

    def take_i(s, _):
        a = stage[16 + s]
        owner, k = owner_of(a), within(a)
        here = same_rows(lax.shift_right_logical(owner, 3), yhi)
        for f in range(5):
            far_i[f, pl.ds(s, 1), :] = jnp.where(
                here, cent_i[owner & 7, f, pl.ds(k, 1), :], got_i[f, pl.ds(s, 1), :]
            )
        return 0

    lax.fori_loop(0, NFAR, take_i, 0)
    y_copies[1].wait_recv()

    def take_j(s, _):
        b = stage[32 + s]
        owner, k = owner_of(b), within(b)
        here = same_rows(owner & 1, ylo)
        for f in range(5):
            far_j[f, pl.ds(s, 1), :] = jnp.where(
                here, cent_j[lax.shift_right_logical(owner, 1), f, pl.ds(k, 1), :], got_j[f, pl.ds(s, 1), :]
            )
        return 0

    lax.fori_loop(0, NFAR, take_j, 0)

    for copy in near_copies:
        copy.wait_recv()

    def take_near(s, _):
        owner = owner_of(stage[NNEAR + 1 + s])
        near_out[s] = nrecv[owner, s]
        near_dens[pl.ds(s, 1), :] = nrecvd[owner, pl.ds(s, 1), :]
        return 0

    lax.fori_loop(0, NREM, take_near, 0)
    near_dens[NREM:, :] = jnp.zeros((8 - NREM, BLK), F32)
    for copy in list_copies + x_copies + relays + z_copies + near_copies + y_copies:
        copy.wait_send()


def exchange(pts, dens, npairs, fpairs):
    dma = pltpu.SemaphoreType.DMA
    shape = jax.ShapeDtypeStruct
    return pl.pallas_call(
        exchange_kernel,
        out_shape=(
            shape((NREM, 4, 4, BLK), F32),
            shape((8, BLK), F32),
            shape((5, NFAR, BLK), F32),
            shape((5, NFAR, BLK), F32),
            shape((BPD, BLK), F32),
        ),
        in_specs=[pl.BlockSpec(memory_space=pltpu.VMEM)] * 2 + [pl.BlockSpec(memory_space=pltpu.SMEM)] * 2,
        out_specs=[pl.BlockSpec(memory_space=pltpu.VMEM)] * 5,
        scratch_shapes=[
            pltpu.SMEM((N_ROW + 1, LIST), jnp.int32),
            pltpu.SMEM((LIST,), jnp.int32),
            vmem(BPD, 4, 4, BLK),
            vmem(8, 5, BPD, BLK),
            vmem(4, 5, BPD, BLK),
            vmem(5, NFAR, BLK),
            vmem(5, NFAR, BLK),
            vmem(5, NFAR, BLK),
            vmem(5, NFAR, BLK),
            vmem(N_ROW - 1, NREM, 4, 4, BLK),
            vmem(N_ROW - 1, 8, BLK),
            vmem(N_ROW, NREM, 4, 4, BLK),
            vmem(N_ROW, 8, BLK),
            dma((8,)), dma((8,)), dma((7,)), dma((7,)), dma((3,)), dma((3,)),
            dma((7,)), dma((7,)), dma((7,)), dma((7,)), dma((2,)), dma((2,)),
        ],
        compiler_params=pltpu.CompilerParams(collective_id=0, has_side_effects=True, vmem_limit_bytes=40 << 20),
    )(pts, dens, npairs, fpairs)


def split3(v):
    hi = v.astype(BF16).astype(F32)
    rest = v - hi
    mid = rest.astype(BF16).astype(F32)
    return hi, mid, rest - mid


def left_rows(px, py, pz, w):
    inv = 1.0 / (w * w)
    rows = []
    for v in ((px * px + py * py + pz * pz + soft_sq) * inv, inv, -2.0 * px * inv, -2.0 * py * inv, -2.0 * pz * inv):
        hi, mid, lo = split3(v)
        rows += [hi, hi, mid, mid, hi, lo]
    return rows


def right_rows(px, py, pz, w):
    inv = 1.0 / (w * w)
    rows = []
    for v in (inv, (px * px + py * py + pz * pz) * inv, px * inv, py * inv, pz * inv):
        hi, mid, lo = split3(v)
        rows += [hi, mid, hi, mid, lo, hi]
    return rows


def put_rows(ref, rows):
    n = rows[0].shape[0]
    for k, v in enumerate(rows):
        ref[k * n : (k + 1) * n, :] = v


def tile_kernel(
    pts, own_dens, near_pts, near_dens, far_i, far_j, npairs, fpairs, ncount, fcount,
    own_out, row_msg, col_msg,
    abuf, bbuf, lhs, rhs, tile, pj, dj, cfi, cfj, fa, fb,
):
    r = lax.axis_index("row")
    c = lax.axis_index("col")
    own_out[...] = jnp.zeros((BPD, BLK), F32)
    row_msg[...] = jnp.zeros_like(row_msg)
    col_msg[...] = jnp.zeros_like(col_msg)
    abuf[120:, :] = jnp.zeros((8, BLK), F32)
    bbuf[120:, :] = jnp.zeros((8, BLK), F32)
    fa[30:, :] = jnp.zeros((2, BLK), F32)
    fb[30:, :] = jnp.zeros((2, BLK), F32)
    lane = lax.broadcasted_iota(jnp.int32, (BLK, 128), 1) % 4
    ri = lax.broadcasted_iota(jnp.int32, (128, 128), 0)
    ci = lax.broadcasted_iota(jnp.int32, (128, 128), 1)

    def apply(di, dj):
        turned = jnp.transpose(jnp.broadcast_to(di, (128, BLK)))
        part = None
        to_cols = []
        for q in range(4):
            cols = slice(q * 128, (q + 1) * 128)
            blk = tile[:, cols]
            e = blk * dj[:, cols]
            part = e if part is None else part + e
            to_cols.append(jnp.sum(blk * turned, axis=0, keepdims=True))
        to_rows = jnp.sum(jnp.transpose(part), axis=0, keepdims=True)
        return to_rows, jnp.concatenate(to_cols, axis=1)

    def mirrored(a, b):
        same = (b // BPD == r) & (a // BPD == c) & (lax.rem(a, BPD) == lax.rem(b, BPD))
        return jnp.where(same, 0.0, 1.0).astype(F32)

    def near(s, _):
        a, b = npairs[s, 0], npairs[s, 1]
        k = a - c * BPD
        cols = pl.ds(pl.multiple_of(k * BLK, BLK), BLK)

        @pl.when(s == 0)
        def _():
            pj[...] = pts[:, :, cols]
            dj[...] = own_dens[pl.ds(k, 1), :]

        @pl.when(s > 0)
        def _():
            pj[...] = near_pts[s - 1]
            dj[...] = near_dens[pl.ds(s - 1, 1), :]

        left = [pts[d, :, cols] for d in range(4)]
        mid = [jnp.mean(left[d]) for d in range(3)]
        put_rows(abuf, left_rows(*(left[d] - mid[d] for d in range(3)), left[3]))
        put_rows(bbuf, right_rows(*(pj[d] - mid[d] for d in range(3)), pj[3]))
        at = jnp.transpose(abuf[...]).astype(BF16)
        for u in range(4):
            lhs[u] = jnp.where(lane == u, at, jnp.zeros_like(at))
        bt = bbuf[...].astype(BF16)
        rhs[0] = bt
        for t in range(1, 4):
            shift = jnp.where((ri // 4 == ci // 4) & ((ri % 4 + t) % 4 == ci % 4), 1.0, 0.0).astype(BF16)
            rhs[t] = jnp.dot(shift, bt, preferred_element_type=F32).astype(BF16)
        for t in range(4):
            for h in range(2):
                half = slice(h * 256, (h + 1) * 256)
                acc = None
                for u in range(4):
                    v = lax.rsqrt(jnp.dot(lhs[u], rhs[t][:, half], preferred_element_type=F32))
                    acc = v if acc is None else acc + v
                if t == 0:
                    tile[:, half] = acc
                else:
                    tile[:, half] += acc
        to_rows, to_cols = apply(own_dens[pl.ds(k, 1), :], dj[...])
        own_out[pl.ds(k, 1), :] += to_rows
        col_msg[pl.ds(16 + s, 1), :] = mirrored(a, b) * to_cols
        return 0

    lax.fori_loop(0, ncount[0], near, 0)

    for d in range(3):
        mid = jnp.mean(far_i[d], axis=1, keepdims=True)
        cfi[d] = far_i[d] - mid
        cfj[d] = far_j[d] - mid

    def far(s, _):
        a, b = fpairs[s, 0], fpairs[s, 1]
        one = pl.ds(s, 1)
        put_rows(fa, left_rows(*(cfi[d, one, :] for d in range(3)), far_i[3, one, :]))
        put_rows(fb, right_rows(*(cfj[d, one, :] for d in range(3)), far_j[3, one, :]))
        at = jnp.transpose(fa[...]).astype(BF16)
        bt = fb[...].astype(BF16)
        for h in range(2):
            half = slice(h * 256, (h + 1) * 256)
            tile[:, half] = lax.rsqrt(jnp.dot(at, bt[:, half], preferred_element_type=F32))
        to_rows, to_cols = apply(far_i[4, one, :], far_j[4, one, :])
        row_msg[one, :] = to_rows
        col_msg[one, :] = mirrored(a, b) * to_cols
        return 0

    lax.fori_loop(0, fcount[0], far, 0)

    at_lane = lax.broadcasted_iota(jnp.int32, (1, BLK), 1)
    ids_a = jnp.full((1, BLK), -1, jnp.int32)
    ids_b = jnp.full((1, BLK), -1, jnp.int32)
    for s in range(NFAR):
        ids_a = jnp.where(at_lane == s, fpairs[s, 0], ids_a)
        ids_b = jnp.where(at_lane == s, fpairs[s, 1], ids_b)
    for s in range(NNEAR):
        ids_b = jnp.where(at_lane == 16 + s, npairs[s, 1], ids_b)
    row_msg[16:17, :] = ids_a.astype(F32)
    col_msg[22:23, :] = ids_b.astype(F32)


def tiles(pts, own_dens, near_pts, near_dens, far_i, far_j, npairs, fpairs, ncount, fcount):
    shape = jax.ShapeDtypeStruct
    return pl.pallas_call(
        tile_kernel,
        out_shape=(shape((BPD, BLK), F32), shape((24, BLK), F32), shape((24, BLK), F32)),
        in_specs=[pl.BlockSpec(memory_space=pltpu.VMEM)] * 6 + [pl.BlockSpec(memory_space=pltpu.SMEM)] * 4,
        out_specs=[pl.BlockSpec(memory_space=pltpu.VMEM)] * 3,
        scratch_shapes=[
            vmem(128, BLK),
            vmem(128, BLK),
            vmem(4, BLK, 128, dtype=BF16),
            vmem(4, 128, BLK, dtype=BF16),
            vmem(BLK, BLK),
            vmem(4, 4, BLK),
            vmem(1, BLK),
            vmem(3, NFAR, BLK),
            vmem(3, NFAR, BLK),
            vmem(32, BLK),
            vmem(32, BLK),
        ],
        compiler_params=pltpu.CompilerParams(vmem_limit_bytes=40 << 20),
    )(pts, own_dens, near_pts, near_dens, far_i, far_j, npairs, fpairs, ncount, fcount)


def scatter(ids, base, count, vals):
    place = lax.broadcasted_iota(jnp.int32, (count, 24), 0) + base
    hot = jnp.where(place == ids, 1.0, 0.0).astype(BF16)
    out = None
    for part in split3(vals):
        v = jnp.dot(hot, part.astype(BF16), preferred_element_type=F32)
        out = v if out is None else out + v
    return out


def collect_kernel(
    own, row_msg, col_msg, out,
    row_got, col_got, half, parts, ysend, yrecv, csend, crecv, psend, precv,
):
    r = lax.axis_index("row")
    c = lax.axis_index("col")
    yhi, xc = c // 8, lax.rem(c, 8)
    y_far = (r, lax.rem(c + 8, N_COL))
    row_peers = [(lax.rem(r + i, N_ROW), c) for i in range(1, N_ROW)]
    x_peers = [(r, yhi * 8 + lax.rem(xc + i, 8)) for i in range(1, 8)]
    barrier = pltpu.get_barrier_semaphore()
    everyone = row_peers + x_peers + [y_far]
    for p in everyone:
        pl.semaphore_signal(barrier, inc=1, device_id=p, device_id_type=MESH)
    pl.semaphore_wait(barrier, len(everyone))

    def remote(src, dst, send, recv, peer):
        copy = pltpu.make_async_remote_copy(
            src_ref=src, dst_ref=dst, send_sem=send, recv_sem=recv, device_id=peer, device_id_type=MESH
        )
        copy.start()
        return copy

    y_copy = remote(row_msg, row_got, ysend.at[0], yrecv.at[0], y_far)
    c_copies = [remote(col_msg, col_got.at[i], csend.at[i], crecv.at[i], p) for i, p in enumerate(row_peers)]

    def rows_of(msg):
        return scatter(msg[16:17, 0:24].astype(jnp.int32), yhi * 128, 128, msg[...])

    mine = rows_of(row_msg)
    y_copy.wait_recv()
    total = mine + rows_of(row_got)
    for g in range(8):
        half[g] = total[g * BPD : (g + 1) * BPD, :]
    p_copies = []
    for i, p in enumerate(x_peers):
        to = lax.rem(xc + 1 + i, 8)
        p_copies.append(remote(half.at[to], parts.at[i], psend.at[i], precv.at[i], p))
    acc = own[...] + half[xc]

    def cols_of(msg):
        return scatter(msg[22:23, 0:24].astype(jnp.int32), r * BPD, BPD, msg[...])

    acc = acc + cols_of(col_msg)
    for i, copy in enumerate(c_copies):
        copy.wait_recv()
        acc = acc + cols_of(col_got.at[i])
    for i, copy in enumerate(p_copies):
        copy.wait_recv()
        acc = acc + parts[i]
    for q in range(4):
        out[pl.ds(q, BPD, stride=4), :] = acc[:, q * 128 : (q + 1) * 128]
    for copy in [y_copy] + c_copies + p_copies:
        copy.wait_send()


def collect(own, row_msg, col_msg):
    dma = pltpu.SemaphoreType.DMA
    return pl.pallas_call(
        collect_kernel,
        out_shape=jax.ShapeDtypeStruct((BPD * 4, 128), F32),
        in_specs=[pl.BlockSpec(memory_space=pltpu.VMEM)] * 3,
        out_specs=pl.BlockSpec(memory_space=pltpu.VMEM),
        scratch_shapes=[
            vmem(24, BLK),
            vmem(N_ROW - 1, 24, BLK),
            vmem(8, BPD, BLK),
            vmem(7, BPD, BLK),
            dma((1,)), dma((1,)), dma((7,)), dma((7,)), dma((7,)), dma((7,)),
        ],
        compiler_params=pltpu.CompilerParams(collective_id=1, has_side_effects=True, vmem_limit_bytes=16 << 20),
    )(own, row_msg, col_msg)


def body(points, density, near_pairs, far_pairs, near_count, far_count):
    near_pts, near_dens, far_i, far_j, own_dens = exchange(points, density.reshape(-1, 128), near_pairs, far_pairs)
    own, row_msg, col_msg = tiles(
        points, own_dens, near_pts, near_dens, far_i, far_j, near_pairs, far_pairs, near_count, far_count
    )
    return collect(own, row_msg, col_msg).reshape(-1)


def solution(mesh):
    in_specs = (
        P(None, None, ("row", "col")),
        P(("row", "col")),
        P(("row", "col"), None),
        P(("row", "col"), None),
        P(("row", "col")),
        P(("row", "col")),
    )
    out_specs = P(("row", "col"))
    return jax.shard_map(body, mesh=mesh, in_specs=in_specs, out_specs=out_specs, check_vma=False)
```

time: 742 us -> 71.4 us (0.10)
  waiting for transfers between devices: 532 us -> 0 us
  Pallas kernels: 0 us -> 64.9 us
  blocking collectives: 57.7 us -> 0 us
  loops' own time: 45 us -> 0 us
  other arithmetic: 42.7 us -> 0 us
  local copies, waits for them, and re-layouts: 23.3 us -> 3.85 us
  matrix products: 18.5 us -> 0 us
  between operations: 14.6 us -> 1.33 us
    unnamed x6 -> x0, waiting for transfers between devices: 476 us -> none
    pallas_call x0 -> x3, Pallas kernels: none -> 64.9 us  [the longest x1 34.6 us: exchange(): pl.pallas_call(exchange_kernel, out_shape=(shape((NREM, 4, 4, BLK), F32),...]
    all_gather x2 -> x0, blocking collectives: 57.7 us -> none  [the longest x1 31.5 us: body(): lax.all_gather(density, 'row', axis=0, tiled=True)]
    all_gather x2 -> x0, waiting for transfers between devices: 55.7 us -> none  [the longest x1 42.1 us: body(): lax.all_gather(points, 'row', axis=2, tiled=True)]
    another operation x2 -> x0, loops' own time: 45 us -> none  [the longest x1 26.7 us: body(): row_acc, col_acc = lax.fori_loop(0, far_count[0], far_step, acc)]
    dot_general x10 -> x0, matrix products: 18.5 us -> none  [the longest x5 11.9 us: accumulate(): to_rows = jnp.dot(tile, dens_b, precision=lax.Precision.HIGHEST)]
    add x3 -> x0, other arithmetic: 17 us -> none  [the longest x2 15.6 us: near_tile(): total + left[3, u][:, None] * right[3, v][None, :] * lax.rsqrt(dist + sof...]
    reduce_sum x2 -> x0, other arithmetic: 11.8 us -> none  [centroids(): place = jnp.sum(blocked[:3] * blocked[3][None], axis=1) / weight[None]]
  transfers between devices with their start and end apart: 4 -> 0, of which waited for: 4 -> 0; matrix products, arithmetic and copies ran while one was open for 6% -> 0% of each run, Pallas kernels for 0% -> 0%
where the time goes in v1:
time: 71.4 us; the launch traced here: 70.1 us
  Pallas kernels  64.9 us (91%)
  local copies, waits for them, and re-layouts  3.85 us (5%)
  between operations  1.33 us (2%)
    pallas_call x1, Pallas kernels, exchange(): pl.pallas_call(exchange_kernel, out_shape=(shape((NREM, 4, 4, BLK), F32),...  34.6 us
    pallas_call x1, Pallas kernels, collect(): pl.pallas_call(collect_kernel, out_shape=jax.ShapeDtypeStruct((BPD * 4, 1...  21.9 us
    pallas_call x1, Pallas kernels, tiles(): pl.pallas_call(tile_kernel, out_shape=(shape((BPD, BLK), F32), shape((24,...  8.4 us
    unnamed x11, local copies, waits for them, and re-layouts  3.85 us

profile of v1, /device:TPU:0, one launch (start us, length us, event | category | flops | bytes accessed | tf_op | source)
XLA Modules:
  0.0 70.1 jit_solution(15218725015286325127)
XLA Ops:
  1.3 0.0 copy-start.2
  1.3 0.7 copy-done.2
  2.0 0.0 copy-start.3
  2.0 0.1 copy.7.npairs
  2.1 0.6 copy-done.3
  2.7 0.1 copy.8.fpairs
  2.7 0.0 copy-start
  2.7 1.0 %copy-done = f32[4,4,8192]{2,1,0:T(4,128)S(1)} copy-done((f32[4,4,8192]{2,1,0:T(4,128)S(1)}, f32[4,4,8192]{2,1,0:T(4,128)}, u32[]{:S(2)}) %copy-start) | copy-done | bytes 524312
  3.8 0.0 copy-start.1
  3.8 0.8 %copy-done.1 = f32[8192]{0:T(1024)S(1)} copy-done((f32[8192]{0:T(1024)S(1)}, f32[8192]{0:T(1024)}, u32[]{:S(2)}) %copy-start.1) | copy-done | bytes 32792
  4.5 34.6 %shard_map.64 = (f32[5,4,4,512]{3,2,1,0:T(4,128)S(1)}, f32[8,512]{1,0:T(8,128)S(1)}, f32[5,16,512]{2,1,0:T(8,128)S(1)}, f32[5,16,512]{2,1,0:T(8,128)S(1)}, f32[16,512]{1,0:T(8,128)S(1)}) custom-call(f32[4,4,8192]{2,1,0:T(4,128)S(1)} %copy-done, f32[64,128]{1,0:T(8,128)S(1)} %bitcast.3, s32[6,2]{1,0:T(8,128)S(1)} %copy.7.npairs, s32[16,2]{1,0:T(8,128)S(1)} %copy.8.fpairs), custom_call_target="tpu_custom_call" | custom-call | tf_op jit(solution)/shard_map/pallas_call | solution.py:206
  39.1 8.4 %shard_map.65 = (f32[16,512]{1,0:T(8,128)S(1)}, f32[24,512]{1,0:T(8,128)S(1)}, f32[24,512]{1,0:T(8,128)S(1)}) custom-call(f32[4,4,8192]{2,1,0:T(4,128)S(1)} %copy-done, f32[16,512]{1,0:T(8,128)S(1)} %get-tuple-element.13.own_dens, f32[5,4,4,512]{3,2,1,0:T(4,128)S(1)} %get-tuple-element.14.near_pts, f32[8,512]{1,0:T(8,128)S(1)} %get-tuple-element.15.near_dens, ...), custom_call_target="tpu_custom_call" | custom-call | tf_op jit(solution)/shard_map/pallas_call | solution.py:385
  47.5 21.9 %shard_map.66 = f32[64,128]{1,0:T(8,128)S(1)} custom-call(f32[16,512]{1,0:T(8,128)S(1)} %get-tuple-element.18.own, f32[24,512]{1,0:T(8,128)S(1)} %get-tuple-element.19.row_msg, f32[24,512]{1,0:T(8,128)S(1)} %get-tuple-element.20.col_msg), custom_call_target="tpu_custom_call" | custom-call | tf_op jit(solution)/shard_map/pallas_call | solution.py:475
  69.4 0.6 copy.14
Async XLA Ops:
  1.3 0.7 copy-start.2
  2.0 0.7 copy-start.3
  2.7 1.0 %copy-start = (f32[4,4,8192]{2,1,0:T(4,128)S(1)}, f32[4,4,8192]{2,1,0:T(4,128)}, u32[]{:S(2)}) copy-start(f32[4,4,8192]{2,1,0:T(4,128)} %pts.3) | copy-start | bytes 1572868
  3.8 0.8 %copy-start.1 = (f32[8192]{0:T(1024)S(1)}, f32[8192]{0:T(1024)}, u32[]{:S(2)}) copy-start(f32[8192]{0:T(1024)} %param.7) | copy-start | bytes 98308

commit v2 on v0

v2 whole, which is shorter than its diff:
```python
import jax
import jax.numpy as jnp
from jax import lax
from jax.experimental import pallas as pl
from jax.experimental.pallas import tpu as pltpu
from jax.sharding import PartitionSpec as P

BLK = 512
BPD = 16
NNEAR = 6
NFAR = 16
N_ROW = 8
N_COL = 16
soft_sq = 0.0004

MESH = pl.DeviceIdType.MESH
F32 = jnp.float32
BF16 = jnp.bfloat16
NREM = NNEAR - 1
LIST = 64


def vmem(*shape, dtype=F32):
    return pltpu.VMEM(shape, dtype)


def owner_of(block):
    return lax.shift_right_logical(block, 4)


def within(block):
    return block & (BPD - 1)


def row_mask(a, b, op):
    return op(jnp.full((1, BLK), a, jnp.int32), jnp.full((1, BLK), b, jnp.int32))


def same_rows(a, b):
    return row_mask(a, b, lambda x, y: x == y)


def split3(v):
    hi = v.astype(BF16).astype(F32)
    rest = v - hi
    mid = rest.astype(BF16).astype(F32)
    return hi, mid, rest - mid


def left_rows(px, py, pz, w):
    inv = 1.0 / (w * w)
    rows = []
    for v in ((px * px + py * py + pz * pz + soft_sq) * inv, inv, -2.0 * px * inv, -2.0 * py * inv, -2.0 * pz * inv):
        hi, mid, lo = split3(v)
        rows += [hi, hi, mid, mid, hi, lo]
    return rows


def right_rows(px, py, pz, w):
    inv = 1.0 / (w * w)
    rows = []
    for v in (inv, (px * px + py * py + pz * pz) * inv, px * inv, py * inv, pz * inv):
        hi, mid, lo = split3(v)
        rows += [hi, mid, hi, mid, lo, hi]
    return rows


def put_rows(ref, rows):
    n = rows[0].shape[0]
    for k, v in enumerate(rows):
        ref[k * n : (k + 1) * n, :] = v


def scatter(ids, base, count, vals):
    place = lax.broadcasted_iota(jnp.int32, (count, vals.shape[0]), 0) + base
    hot = jnp.where(place == ids, 1.0, 0.0).astype(BF16)
    out = None
    for part in split3(vals):
        v = jnp.dot(hot, part.astype(BF16), preferred_element_type=F32)
        out = v if out is None else out + v
    return out


def gathered(msgs, base, count, at):
    m, n, _ = msgs.shape
    ids = jnp.concatenate([msgs[i, at : at + 1, 0:n] for i in range(m)], axis=1).astype(jnp.int32)
    return scatter(ids, base, count, msgs[...].reshape(m * n, BLK))


def potential_kernel(
    pts_hbm, dens_hbm, npairs, fpairs, ncount, fcount,
    out,
    lists, stage, blocks, dens, cent_i, cent_j, own_dens, sel_i, sel_j, got_i, got_j, far_i, far_j,
    pack, packd, nrecv, nrecvd,
    abuf, bbuf, left, turned, mids, lhs, rhs, tile, pj, fa, fb,
    rows_all, cols_all, near_all, half, parts,
    load, lsend, lrecv, xsend, xrecv, zsend, zrecv, nsend, nrcv, dsend, drcv, ysend, yrecv,
    msend, mrecv, fsend, frecv, csend, crecv, psend, precv,
):
    r = lax.axis_index("row")
    c = lax.axis_index("col")
    z, ylo = r // 2, lax.rem(r, 2)
    yhi, xc = c // 8, lax.rem(c, 8)
    x, core = xc // 2, lax.rem(xc, 2)
    row_peers = [(lax.rem(r + i, N_ROW), c) for i in range(1, N_ROW)]
    xc_peers = [(r, yhi * 8 + lax.rem(xc + i, 8)) for i in range(1, 8)]
    x_peers = [(r, yhi * 8 + lax.rem(x + i, 4) * 2 + core) for i in range(1, 4)]
    core_peer = (r, yhi * 8 + x * 2 + 1 - core)
    y_far = (r, lax.rem(c + 8, N_COL))
    y_near = (r + 1 - 2 * ylo, c)

    barrier = pltpu.get_barrier_semaphore()
    everyone = row_peers + xc_peers + [y_far]
    for p in everyone:
        pl.semaphore_signal(barrier, inc=1, device_id=p, device_id_type=MESH)

    loads = [
        pltpu.make_async_copy(pts_hbm.at[:, :, pl.ds(k * BLK, BLK)], blocks.at[k], load.at[k]) for k in range(BPD)
    ]
    loads.append(pltpu.make_async_copy(dens_hbm, dens, load.at[BPD]))
    for copy in loads:
        copy.start()

    for s in range(NNEAR):
        stage[s] = npairs[0, s]
        stage[NNEAR + s] = npairs[1, s]
    for s in range(NFAR):
        stage[16 + s] = fpairs[0, s]
        stage[32 + s] = fpairs[1, s]
    abuf[120:, :] = jnp.zeros((8, BLK), F32)
    bbuf[120:, :] = jnp.zeros((8, BLK), F32)
    fa[30:, :] = jnp.zeros((2, BLK), F32)
    fb[30:, :] = jnp.zeros((2, BLK), F32)
    for copy in loads:
        copy.wait()

    def centroid(k, _):
        p = blocks[k]
        w = p[3]
        total = jnp.sum(w, axis=0, keepdims=True)
        for d in range(3):
            cent_i[xc, d, pl.ds(k, 1), :] = jnp.sum(p[d] * w, axis=0, keepdims=True) / total
        cent_i[xc, 3, pl.ds(k, 1), :] = total
        return 0

    lax.fori_loop(0, BPD, centroid, 0)
    for q in range(4):
        own_dens[:, q * 128 : (q + 1) * 128] = dens[pl.ds(q, BPD, stride=4), :]
    cent_i[xc, 4] = own_dens[...]
    cent_j[z] = cent_i[xc]

    pl.semaphore_wait(barrier, len(everyone))

    def remote(src, dst, send, recv, peer):
        return pltpu.make_async_remote_copy(
            src_ref=src, dst_ref=dst, send_sem=send, recv_sem=recv, device_id=peer, device_id_type=MESH
        )

    started = []

    def go(copy):
        copy.start()
        started.append(copy)
        return copy

    list_copies = [go(remote(stage, lists.at[r], lsend.at[i], lrecv.at[i], p)) for i, p in enumerate(row_peers)]
    list_copies.append(go(remote(stage, lists.at[N_ROW], lsend.at[7], lrecv.at[7], y_far)))
    x_copies = [go(remote(cent_i.at[xc], cent_i.at[xc], xsend.at[i], xrecv.at[i], p)) for i, p in enumerate(x_peers)]
    x_copies.append(go(remote(cent_i.at[xc], cent_i.at[xc], xsend.at[3], xrecv.at[3], core_peer)))
    z_copies = [
        go(remote(cent_j.at[z], cent_j.at[z], zsend.at[i - 1], zrecv.at[i - 1], (lax.rem(z + i, 4) * 2 + ylo, c)))
        for i in range(1, 4)
    ]

    lane = lax.broadcasted_iota(jnp.int32, (BLK, 128), 1) % 4
    ri = lax.broadcasted_iota(jnp.int32, (128, 128), 0)
    ci = lax.broadcasted_iota(jnp.int32, (128, 128), 1)

    def turn(di):
        return jnp.transpose(jnp.broadcast_to(di, (128, BLK)))

    def apply(column, dj):
        part = None
        to_cols = []
        for q in range(4):
            cols = slice(q * 128, (q + 1) * 128)
            blk = tile[:, cols]
            e = blk * dj[:, cols]
            part = e if part is None else part + e
            to_cols.append(jnp.sum(blk * column, axis=0, keepdims=True))
        to_rows = jnp.sum(jnp.transpose(part), axis=0, keepdims=True)
        return to_rows, jnp.concatenate(to_cols, axis=1)

    def masks(a, b, s, count):
        used = row_mask(s, count, lambda m, n: m < n)
        other = row_mask((b ^ (r * BPD + within(a))) | (owner_of(a) ^ c), 0, lambda m, n: m != n)
        return used, used & other

    def near_left(s, _):
        k = within(stage[s])
        p = blocks[k]
        mid = [jnp.mean(p[d]) for d in range(3)]
        put_rows(abuf, left_rows(*(p[d] - mid[d] for d in range(3)), p[3]))
        left[s] = jnp.transpose(abuf[...]).astype(BF16)
        turned[s] = turn(own_dens[pl.ds(k, 1), :])
        for d in range(3):
            mids[s, d : d + 1, :] = jnp.full((1, BLK), mid[d], F32)
        return 0

    def near_right(s, p, dj):
        put_rows(bbuf, right_rows(*(p[d] - mids[s, d : d + 1, :] for d in range(3)), p[3]))
        bt = bbuf[...].astype(BF16)
        rhs[0] = bt
        for t in range(1, 4):
            shift = jnp.where((ri // 4 == ci // 4) & ((ri % 4 + t) % 4 == ci % 4), 1.0, 0.0).astype(BF16)
            rhs[t] = jnp.dot(shift, bt, preferred_element_type=F32).astype(BF16)
        at = left[s]
        for u in range(4):
            lhs[u] = jnp.where(lane == u, at, jnp.zeros_like(at))
        for t in range(4):
            for h in range(2):
                span = slice(h * 256, (h + 1) * 256)
                acc = None
                for u in range(4):
                    v = lax.rsqrt(jnp.dot(lhs[u], rhs[t][:, span], preferred_element_type=F32))
                    acc = v if acc is None else acc + v
                if t == 0:
                    tile[:, span] = acc
                else:
                    tile[:, span] += acc
        to_rows, to_cols = apply(turned[s], dj)
        used, mirror = masks(stage[s], stage[NNEAR + s], s, ncount[0])
        near_all[8, pl.ds(s, 1), :] = jnp.where(used, to_rows, 0.0)
        near_all[7, pl.ds(s, 1), :] = jnp.where(mirror, to_cols, 0.0)

    def near_copy(i, s):
        peer = lax.rem(r + i, N_ROW)
        return remote(pack.at[i - 1, s], nrecv.at[s, r], nsend.at[i - 1, s], nrcv.at[i - 1, s], (peer, c))

    def near_slot(s):
        for i in range(1, N_ROW):
            near_copy(i, s).wait_recv()
        b = stage[NNEAR + 1 + s]
        owner = owner_of(b)
        p = nrecv[s, 0]
        d = nrecvd[0, pl.ds(s, 1), :]
        for o in range(1, N_ROW):
            hit = jnp.full((4, 4, BLK), owner, jnp.int32) == o
            p = jnp.where(hit, nrecv[s, o], p)
            d = jnp.where(same_rows(owner, o), nrecvd[o, pl.ds(s, 1), :], d)
        pj[...] = p
        near_right(s + 1, pj, d)

    for m in range(7, 9):
        near_all[m] = jnp.zeros((8, BLK), F32)
    lax.fori_loop(0, NNEAR, near_left, 0)

    for copy in list_copies:
        copy.wait_recv()
    dens_copies = []
    for i in range(N_ROW):
        peer = lax.rem(r + i, N_ROW)
        source = stage if i == 0 else lists.at[peer]
        for s in range(NREM):
            row = own_dens[pl.ds(within(source[NNEAR + 1 + s]), 1), :]
            if i == 0:
                nrecvd[r, s : s + 1, :] = row
            else:
                packd[i - 1, s : s + 1, :] = row
        if i > 0:
            packd[i - 1, NREM:, :] = jnp.zeros((8 - NREM, BLK), F32)
            dens_copies.append(go(remote(packd.at[i - 1], nrecvd.at[r], dsend.at[i - 1], drcv.at[i - 1], (peer, c))))

    def fill(s, _):
        nrecv[s, r] = blocks[within(stage[NNEAR + 1 + s])]
        for i in range(1, N_ROW):
            pack[i - 1, s] = blocks[within(lists[lax.rem(r + i, N_ROW), NNEAR + 1 + s])]
            near_copy(i, s).start()
        return 0

    lax.fori_loop(0, NREM, fill, 0)

    k0 = within(stage[0])
    pj[...] = blocks[k0]
    near_right(0, pj, own_dens[pl.ds(k0, 1), :])

    relays = []
    for i in range(1, 4):
        x_copies[i - 1].wait_recv()
        g = lax.rem(x - i + 4, 4) * 2 + core
        relays.append(go(remote(cent_i.at[g], cent_i.at[g], xsend.at[3 + i], xrecv.at[3 + i], core_peer)))
    for copy in z_copies:
        copy.wait_recv()
    near_row = y_near[0]

    def choose_j(s, _):
        b = lists[near_row, 32 + s]
        g, k = lax.shift_right_logical(owner_of(b), 1), within(b)
        for f in range(5):
            sel_j[f, pl.ds(s, 1), :] = cent_j[g, f, pl.ds(k, 1), :]
        return 0

    lax.fori_loop(0, NFAR, choose_j, 0)
    yj_copy = go(remote(sel_j, got_j, ysend.at[1], yrecv.at[1], y_near))
    x_copies[3].wait_recv()
    for copy in relays:
        copy.wait_recv()

    def choose_i(s, _):
        a = lists[N_ROW, 16 + s]
        g, k = owner_of(a) & 7, within(a)
        for f in range(5):
            sel_i[f, pl.ds(s, 1), :] = cent_i[g, f, pl.ds(k, 1), :]
        return 0

    lax.fori_loop(0, NFAR, choose_i, 0)
    yi_copy = go(remote(sel_i, got_i, ysend.at[0], yrecv.at[0], y_far))

    for copy in dens_copies:
        copy.wait_recv()
    near_slot(0)

    yj_copy.wait_recv()
    yi_copy.wait_recv()

    def take(s, _):
        a, b = stage[16 + s], stage[32 + s]
        owner, k = owner_of(a), within(a)
        here = same_rows(lax.shift_right_logical(owner, 3), yhi)
        one = pl.ds(s, 1)
        for f in range(5):
            far_i[f, one, :] = jnp.where(here, cent_i[owner & 7, f, pl.ds(k, 1), :], got_i[f, one, :])
        owner, k = owner_of(b), within(b)
        here = same_rows(owner & 1, ylo)
        for f in range(5):
            far_j[f, one, :] = jnp.where(
                here, cent_j[lax.shift_right_logical(owner, 1), f, pl.ds(k, 1), :], got_j[f, one, :]
            )
        return 0

    lax.fori_loop(0, NFAR, take, 0)
    for d in range(3):
        mid = jnp.mean(far_i[d], axis=1, keepdims=True)
        far_i[d] = far_i[d] - mid
        far_j[d] = far_j[d] - mid

    at_lane = lax.broadcasted_iota(jnp.int32, (1, BLK), 1)

    def ids_of(values, n):
        ids = jnp.full((1, BLK), -1, jnp.int32)
        for s in range(n):
            ids = jnp.where(at_lane == s, values(s), ids)
        return ids.astype(F32)

    for ref, first in ((rows_all.at[0], 16), (cols_all.at[7], 32)):
        ref[16:, :] = jnp.zeros((8, BLK), F32)
        ref[16:17, :] = ids_of(lambda s, first=first: stage[first + s], NFAR)

    def far(s, _):
        one = pl.ds(s, 1)
        put_rows(fa, left_rows(*(far_i[d, one, :] for d in range(4))))
        put_rows(fb, right_rows(*(far_j[d, one, :] for d in range(4))))
        at = jnp.transpose(fa[...]).astype(BF16)
        bt = fb[...].astype(BF16)
        for h in range(2):
            span = slice(h * 256, (h + 1) * 256)
            tile[:, span] = lax.rsqrt(jnp.dot(at, bt[:, span], preferred_element_type=F32))
        to_rows, to_cols = apply(turn(far_i[4, one, :]), far_j[4, one, :])
        used, mirror = masks(stage[16 + s], stage[32 + s], s, fcount[0])
        rows_all[0, one, :] = jnp.where(used, to_rows, 0.0)
        cols_all[7, one, :] = jnp.where(mirror, to_cols, 0.0)
        return 0

    lax.fori_loop(0, NFAR, far, 0)
    m_copy = go(remote(rows_all.at[0], rows_all.at[1], msend.at[0], mrecv.at[0], y_far))
    f_copies = [
        go(remote(cols_all.at[7], cols_all.at[i], fsend.at[i], frecv.at[i], p)) for i, p in enumerate(row_peers)
    ]

    near_slot(1)

    m_copy.wait_recv()
    total = gathered(rows_all, yhi * 128, 128, 16)
    for g in range(8):
        half[g] = total[g * BPD : (g + 1) * BPD, :]
    p_copies = []
    for i, p in enumerate(xc_peers):
        to = lax.rem(xc + 1 + i, 8)
        p_copies.append(go(remote(half.at[to], parts.at[i], psend.at[i], precv.at[i], p)))

    lax.fori_loop(2, NREM, lambda s, v: (near_slot(s), v)[1], 0)

    near_all[8, 6:7, :] = ids_of(lambda s: within(stage[s]) + r * BPD, NNEAR)
    near_all[7, 6:7, :] = ids_of(lambda s: stage[NNEAR + s], NNEAR)
    c_copies = [
        go(remote(near_all.at[7], near_all.at[i], csend.at[i], crecv.at[i], p)) for i, p in enumerate(row_peers)
    ]
    for copy in f_copies:
        copy.wait_recv()
    acc = half[xc] + gathered(cols_all, r * BPD, BPD, 16)
    for i, copy in enumerate(p_copies):
        copy.wait_recv()
        acc = acc + parts[i]
    for copy in c_copies:
        copy.wait_recv()
    acc = acc + gathered(near_all, r * BPD, BPD, 6)
    for q in range(4):
        out[pl.ds(q, BPD, stride=4), :] = acc[:, q * 128 : (q + 1) * 128]
    for copy in started:
        copy.wait_send()

    def sent(s, _):
        for i in range(1, N_ROW):
            near_copy(i, s).wait_send()
        return 0

    lax.fori_loop(0, NREM, sent, 0)


def body(points, density, near_pairs, far_pairs, near_count, far_count):
    dma = pltpu.SemaphoreType.DMA
    smem = pl.BlockSpec(memory_space=pltpu.SMEM)
    hbm = pl.BlockSpec(memory_space=pltpu.HBM)
    out = pl.pallas_call(
        potential_kernel,
        out_shape=jax.ShapeDtypeStruct((BPD * 4, 128), F32),
        in_specs=[hbm, hbm, smem, smem, smem, smem],
        out_specs=pl.BlockSpec(memory_space=pltpu.VMEM),
        scratch_shapes=[
            pltpu.SMEM((N_ROW + 1, LIST), jnp.int32),
            pltpu.SMEM((LIST,), jnp.int32),
            vmem(BPD, 4, 4, BLK),
            vmem(BPD * 4, 128),
            vmem(8, 5, BPD, BLK),
            vmem(4, 5, BPD, BLK),
            vmem(BPD, BLK),
            vmem(5, NFAR, BLK),
            vmem(5, NFAR, BLK),
            vmem(5, NFAR, BLK),
            vmem(5, NFAR, BLK),
            vmem(5, NFAR, BLK),
            vmem(5, NFAR, BLK),
            vmem(N_ROW - 1, NREM, 4, 4, BLK),
            vmem(N_ROW - 1, 8, BLK),
            vmem(NREM, N_ROW, 4, 4, BLK),
            vmem(N_ROW, 8, BLK),
            vmem(128, BLK),
            vmem(128, BLK),
            vmem(NNEAR, BLK, 128, dtype=BF16),
            vmem(NNEAR, BLK, 128),
            vmem(NNEAR, 8, BLK),
            vmem(4, BLK, 128, dtype=BF16),
            vmem(4, 128, BLK, dtype=BF16),
            vmem(BLK, BLK),
            vmem(4, 4, BLK),
            vmem(32, BLK),
            vmem(32, BLK),
            vmem(2, 24, BLK),
            vmem(8, 24, BLK),
            vmem(9, 8, BLK),
            vmem(8, BPD, BLK),
            vmem(7, BPD, BLK),
            dma((BPD + 1,)),
            dma((8,)), dma((8,)), dma((7,)), dma((7,)), dma((3,)), dma((3,)),
            dma((7, NREM)), dma((7, NREM)), dma((7,)), dma((7,)), dma((2,)), dma((2,)),
            dma((1,)), dma((1,)), dma((7,)), dma((7,)), dma((7,)), dma((7,)), dma((7,)), dma((7,)),
        ],
        compiler_params=pltpu.CompilerParams(collective_id=0, has_side_effects=True, vmem_limit_bytes=64 << 20),
    )(points, density.reshape(-1, 128), near_pairs.T, far_pairs.T, near_count, far_count)
    return out.reshape(-1)


def solution(mesh):
    in_specs = (
        P(None, None, ("row", "col")),
        P(("row", "col")),
        P(("row", "col"), None),
        P(("row", "col"), None),
        P(("row", "col")),
        P(("row", "col")),
    )
    out_specs = P(("row", "col"))
    return jax.shard_map(body, mesh=mesh, in_specs=in_specs, out_specs=out_specs, check_vma=False)
```

time: 742 us -> 65.9 us (0.09); the launches traced: 734 us -> 65.6 us
  waiting for transfers between devices: 532 us -> 0 us
  Pallas kernels: 0 us -> 62.9 us
  blocking collectives: 57.7 us -> 0 us
  loops' own time: 45 us -> 0 us
  other arithmetic: 42.7 us -> 0 us
  local copies, waits for them, and re-layouts: 23.3 us -> 1.38 us
  matrix products: 18.5 us -> 0 us
  between operations: 14.6 us -> 1.3 us
    unnamed x6 -> x0, waiting for transfers between devices: 476 us -> none
    pallas_call x0 -> x1, Pallas kernels: none -> 62.9 us  [body(): pl.pallas_call(potential_kernel, out_shape=jax.ShapeDtypeStruct((BPD * 4,...]
    all_gather x2 -> x0, blocking collectives: 57.7 us -> none  [the longest x1 31.5 us: body(): lax.all_gather(density, 'row', axis=0, tiled=True)]
    all_gather x2 -> x0, waiting for transfers between devices: 55.7 us -> none  [the longest x1 42.1 us: body(): lax.all_gather(points, 'row', axis=2, tiled=True)]
    another operation x2 -> x0, loops' own time: 45 us -> none  [the longest x1 26.7 us: body(): row_acc, col_acc = lax.fori_loop(0, far_count[0], far_step, acc)]
    dot_general x10 -> x0, matrix products: 18.5 us -> none  [the longest x5 11.9 us: accumulate(): to_rows = jnp.dot(tile, dens_b, precision=lax.Precision.HIGHEST)]
    add x3 -> x0, other arithmetic: 17 us -> none  [the longest x2 15.6 us: near_tile(): total + left[3, u][:, None] * right[3, v][None, :] * lax.rsqrt(dist + sof...]
    reduce_sum x2 -> x0, other arithmetic: 11.8 us -> none  [centroids(): place = jnp.sum(blocked[:3] * blocked[3][None], axis=1) / weight[None]]
  transfers between devices with their start and end apart: 4 -> 0, of which waited for: 4 -> 0; matrix products, arithmetic and copies ran while one was open for 6% -> 0% of each run, Pallas kernels for 0% -> 0%
where the time goes in v2:
time: 65.9 us; the launch traced here: 65.6 us
  Pallas kernels  62.9 us (95%)
  local copies, waits for them, and re-layouts  1.38 us (2%)
  between operations  1.3 us (2%)
    pallas_call x1, Pallas kernels, body(): pl.pallas_call(potential_kernel, out_shape=jax.ShapeDtypeStruct((BPD * 4,...  62.9 us
    unnamed x1, local copies, waits for them, and re-layouts  1.38 us

profile of v2, /device:TPU:0, one launch (start us, length us, event | category | flops | bytes accessed | tf_op | source)
XLA Modules:
  0.0 65.6 jit_solution(4686079705293730900)
XLA Ops:
  1.3 62.9 %shard_map.64 = f32[64,128]{1,0:T(8,128)} custom-call(f32[4,4,8192]{2,1,0:T(4,128)} %pts_hbm.1, f32[64,128]{1,0:T(8,128)} %bitcast.5, s32[2,6]{1,0:T(2,128)} %bitcast.6, s32[2,16]{1,0:T(2,128)} %bitcast.7, s32[1]{0:T(128)S(6)} %copy.8.ncount, s32[1]{0:T(128)S(6)} %copy.9.fcount), custom_call_target="tpu_custom_call" | custom-call | tf_op jit(solution)/shard_map/pallas_call | solution.py:424
  64.2 1.4 %copy.10 = f32[8192]{0:T(1024)} copy(f32[8192]{0:T(1024)} %bitcast.4) | data formatting | bytes 65536

commit v3 on v2

--- a/solution.py
+++ b/solution.py
@@ -91,10 +91,10 @@
     pts_hbm, dens_hbm, npairs, fpairs, ncount, fcount,
     out,
     lists, stage, blocks, dens, cent_i, cent_j, own_dens, sel_i, sel_j, got_i, got_j, far_i, far_j,
-    pack, packd, nrecv, nrecvd,
+    apack, agot, bpack, bgot, cpack, cgot,
     abuf, bbuf, left, turned, mids, lhs, rhs, tile, pj, fa, fb,
-    rows_all, cols_all, near_all, half, parts,
-    load, lsend, lrecv, xsend, xrecv, zsend, zrecv, nsend, nrcv, dsend, drcv, ysend, yrecv,
+    rows_all, cols_far, near_all, half, parts, side, side_got,
+    load, lsend, lrecv, xsend, xrecv, zsend, zrecv, asend, arecv, bsend, brecv, nsend, nrecv, ysend, yrecv,
     msend, mrecv, fsend, frecv, csend, crecv, psend, precv,
 ):
     r = lax.axis_index("row")
@@ -104,7 +104,9 @@
     x, core = xc // 2, lax.rem(xc, 2)
     row_peers = [(lax.rem(r + i, N_ROW), c) for i in range(1, N_ROW)]
     xc_peers = [(r, yhi * 8 + lax.rem(xc + i, 8)) for i in range(1, 8)]
-    x_peers = [(r, yhi * 8 + lax.rem(x + i, 4) * 2 + core) for i in range(1, 4)]
+    x_up, x_down = [(r, yhi * 8 + lax.rem(x + i, 4) * 2 + core) for i in (1, 3)]
+    zs = [lax.rem(z + i, 4) for i in range(4)]
+    z_up, z_down = (zs[1] * 2 + ylo, c), (zs[3] * 2 + ylo, c)
     core_peer = (r, yhi * 8 + x * 2 + 1 - core)
     y_far = (r, lax.rem(c + 8, N_COL))
     y_near = (r + 1 - 2 * ylo, c)
@@ -124,13 +126,15 @@
     for s in range(NNEAR):
         stage[s] = npairs[0, s]
         stage[NNEAR + s] = npairs[1, s]
+        lists[r, NNEAR + s] = npairs[1, s]
     for s in range(NFAR):
         stage[16 + s] = fpairs[0, s]
         stage[32 + s] = fpairs[1, s]
     abuf[120:, :] = jnp.zeros((8, BLK), F32)
     bbuf[120:, :] = jnp.zeros((8, BLK), F32)
-    fa[30:, :] = jnp.zeros((2, BLK), F32)
-    fb[30:, :] = jnp.zeros((2, BLK), F32)
+    fa[:, 32:, :] = jnp.zeros((2, 16, BLK), F32)
+    fb[:, 30:, :] = jnp.zeros((2, 18, BLK), F32)
+    sel_j[5] = jnp.zeros((NFAR, BLK), F32)
     for copy in loads:
         copy.wait()
 
@@ -165,27 +169,52 @@
 
     list_copies = [go(remote(stage, lists.at[r], lsend.at[i], lrecv.at[i], p)) for i, p in enumerate(row_peers)]
     list_copies.append(go(remote(stage, lists.at[N_ROW], lsend.at[7], lrecv.at[7], y_far)))
-    x_copies = [go(remote(cent_i.at[xc], cent_i.at[xc], xsend.at[i], xrecv.at[i], p)) for i, p in enumerate(x_peers)]
-    x_copies.append(go(remote(cent_i.at[xc], cent_i.at[xc], xsend.at[3], xrecv.at[3], core_peer)))
-    z_copies = [
-        go(remote(cent_j.at[z], cent_j.at[z], zsend.at[i - 1], zrecv.at[i - 1], (lax.rem(z + i, 4) * 2 + ylo, c)))
-        for i in range(1, 4)
-    ]
+    def ring(buf, index, up, down, send, recv):
+        here, above, below = index(0), index(1), index(3)
+        first = [
+            go(remote(buf.at[here], buf.at[here], send.at[0], recv.at[0], up)),
+            go(remote(buf.at[here], buf.at[here], send.at[1], recv.at[1], down)),
+        ]
+
+        def second():
+            low, high = pl.ds(0, 8), pl.ds(8, 8)
+            out = []
+            first[0].wait_recv()
+            out.append(go(remote(buf.at[below, :, low], buf.at[below, :, low], send.at[2], recv.at[2], up)))
+            first[1].wait_recv()
+            out.append(go(remote(buf.at[above, :, high], buf.at[above, :, high], send.at[3], recv.at[3], down)))
+            return out
+
+        return second
+
+    def x_index(i):
+        return lax.rem(x + i, 4) * 2 + core
+
+    x_second = ring(cent_i, x_index, x_up, x_down, xsend, xrecv)
+    z_second = ring(cent_j, lambda i: zs[i], z_up, z_down, zsend, zrecv)
+
+    def to_core(i, sem):
+        part = cent_i.at[x_index(i)]
+        return go(remote(part, part, xsend.at[sem], xrecv.at[sem], core_peer))
+
+    relays = [to_core(0, 4)]
 
     lane = lax.broadcasted_iota(jnp.int32, (BLK, 128), 1) % 4
     ri = lax.broadcasted_iota(jnp.int32, (128, 128), 0)
     ci = lax.broadcasted_iota(jnp.int32, (128, 128), 1)
 
-    def turn(di):
-        return jnp.transpose(jnp.broadcast_to(di, (128, BLK)))
-
-    def apply(column, dj):
+    def spread(turned_rows, first):
+        n = turned_rows.shape[1]
+        k = lax.broadcasted_iota(jnp.int32, (n, 128), 0)
+        pick = jnp.where((k >= first) & (k < first + 3), 1.0, 0.0).astype(BF16)
+        return jnp.dot(turned_rows, pick, preferred_element_type=F32)
+
+    def apply(halves, column, dj):
         part = None
         to_cols = []
         for q in range(4):
-            cols = slice(q * 128, (q + 1) * 128)
-            blk = tile[:, cols]
-            e = blk * dj[:, cols]
+            blk = halves[q // 2][:, (q % 2) * 128 : (q % 2) * 128 + 128]
+            e = blk * dj[:, q * 128 : (q + 1) * 128]
             part = e if part is None else part + e
             to_cols.append(jnp.sum(blk * column, axis=0, keepdims=True))
         to_rows = jnp.sum(jnp.transpose(part), axis=0, keepdims=True)
@@ -201,8 +230,10 @@
         p = blocks[k]
         mid = [jnp.mean(p[d]) for d in range(3)]
         put_rows(abuf, left_rows(*(p[d] - mid[d] for d in range(3)), p[3]))
-        left[s] = jnp.transpose(abuf[...]).astype(BF16)
-        turned[s] = turn(own_dens[pl.ds(k, 1), :])
+        put_rows(abuf.at[120:123], split3(own_dens[pl.ds(k, 1), :]))
+        at = jnp.transpose(abuf[...]).astype(BF16)
+        left[s] = at
+        turned[s] = spread(at, 120)
         for d in range(3):
             mids[s, d : d + 1, :] = jnp.full((1, BLK), mid[d], F32)
         return 0
@@ -228,27 +259,63 @@
                     tile[:, span] = acc
                 else:
                     tile[:, span] += acc
-        to_rows, to_cols = apply(turned[s], dj)
+        to_rows, to_cols = apply([tile.at[:, 0:256], tile.at[:, 256:512]], turned[s], dj)
         used, mirror = masks(stage[s], stage[NNEAR + s], s, ncount[0])
         near_all[8, pl.ds(s, 1), :] = jnp.where(used, to_rows, 0.0)
         near_all[7, pl.ds(s, 1), :] = jnp.where(mirror, to_cols, 0.0)
 
-    def near_copy(i, s):
-        peer = lax.rem(r + i, N_ROW)
-        return remote(pack.at[i - 1, s], nrecv.at[s, r], nsend.at[i - 1, s], nrcv.at[i - 1, s], (peer, c))
+    def wanted(row, s):
+        return lists[row, NNEAR + 1 + s]
+
+    def item_mask(a, b):
+        return jnp.full((4, 4, BLK), a, jnp.int32) == jnp.full((4, 4, BLK), b, jnp.int32)
+
+    def a_copy(way, s):
+        return remote(apack.at[s, way], agot.at[s, way], asend.at[way, s], arecv.at[way, s], (z_up, z_down)[way])
+
+    def b_copy(way, s):
+        return remote(bpack.at[s, way], bgot.at[s, way], bsend.at[way, s], brecv.at[way, s], (z_up, z_down)[way])
+
+    def n_copy(s):
+        return remote(cpack.at[s], cgot.at[s], nsend.at[s], nrecv.at[s], y_near)
+
+    def step_a(s, _):
+        for way in range(2):
+            apack[s, way] = blocks[within(wanted(zs[2] * 2 + way, s))]
+            a_copy(way, s).start()
+        return 0
+
+    def step_b(s, _):
+        for way in range(2):
+            to = zs[1 if way == 0 else 3] * 2
+            bpack[s, way, 1 - way] = blocks[within(wanted(to + 1 - way, s))]
+            b = wanted(to + way, s)
+            a_copy(way, s).wait_recv()
+            bpack[s, way, way] = jnp.where(item_mask(owner_of(b), r), blocks[within(b)], agot[s, way])
+            b_copy(way, s).start()
+        return 0
+
+    def assembled(y, s):
+        b = wanted(z * 2 + y, s)
+        oz = lax.shift_right_logical(owner_of(b), 1)
+        above = (oz ^ zs[1]) * ((oz ^ zs[2]) | (y ^ 1))
+        v = jnp.where(item_mask(above, 0), bgot[s, 1, y], bgot[s, 0, y])
+        return jnp.where(item_mask(oz, z), blocks[within(b)], v)
+
+    def step_c(s, _):
+        for way in range(2):
+            b_copy(way, s).wait_recv()
+        cpack[s] = assembled(1 - ylo, s)
+        n_copy(s).start()
+        return 0
 
     def near_slot(s):
-        for i in range(1, N_ROW):
-            near_copy(i, s).wait_recv()
+        n_copy(s).wait_recv()
         b = stage[NNEAR + 1 + s]
         owner = owner_of(b)
-        p = nrecv[s, 0]
-        d = nrecvd[0, pl.ds(s, 1), :]
-        for o in range(1, N_ROW):
-            hit = jnp.full((4, 4, BLK), owner, jnp.int32) == o
-            p = jnp.where(hit, nrecv[s, o], p)
-            d = jnp.where(same_rows(owner, o), nrecvd[o, pl.ds(s, 1), :], d)
-        pj[...] = p
+        pj[...] = jnp.where(item_mask(owner & 1, ylo), assembled(ylo, s), cgot[s])
+        here = cent_j[lax.shift_right_logical(owner, 1), 4, pl.ds(within(b), 1), :]
+        d = jnp.where(same_rows(owner & 1, ylo), here, got_j[5, pl.ds(s, 1), :])
         near_right(s + 1, pj, d)
 
     for m in range(7, 9):
@@ -257,39 +324,20 @@
 
     for copy in list_copies:
         copy.wait_recv()
-    dens_copies = []
-    for i in range(N_ROW):
-        peer = lax.rem(r + i, N_ROW)
-        source = stage if i == 0 else lists.at[peer]
-        for s in range(NREM):
-            row = own_dens[pl.ds(within(source[NNEAR + 1 + s]), 1), :]
-            if i == 0:
-                nrecvd[r, s : s + 1, :] = row
-            else:
-                packd[i - 1, s : s + 1, :] = row
-        if i > 0:
-            packd[i - 1, NREM:, :] = jnp.zeros((8 - NREM, BLK), F32)
-            dens_copies.append(go(remote(packd.at[i - 1], nrecvd.at[r], dsend.at[i - 1], drcv.at[i - 1], (peer, c))))
-
-    def fill(s, _):
-        nrecv[s, r] = blocks[within(stage[NNEAR + 1 + s])]
-        for i in range(1, N_ROW):
-            pack[i - 1, s] = blocks[within(lists[lax.rem(r + i, N_ROW), NNEAR + 1 + s])]
-            near_copy(i, s).start()
-        return 0
-
-    lax.fori_loop(0, NREM, fill, 0)
+    lax.fori_loop(0, NREM, step_a, 0)
+    x_half = x_second()
+    z_half = z_second()
+    relays += [to_core(3, 5), to_core(1, 6)]
 
     k0 = within(stage[0])
     pj[...] = blocks[k0]
     near_right(0, pj, own_dens[pl.ds(k0, 1), :])
 
-    relays = []
-    for i in range(1, 4):
-        x_copies[i - 1].wait_recv()
-        g = lax.rem(x - i + 4, 4) * 2 + core
-        relays.append(go(remote(cent_i.at[g], cent_i.at[g], xsend.at[3 + i], xrecv.at[3 + i], core_peer)))
-    for copy in z_copies:
+    lax.fori_loop(0, NREM, step_b, 0)
+    for copy in x_half:
+        copy.wait_recv()
+    relays.append(to_core(2, 7))
+    for copy in z_half:
         copy.wait_recv()
     near_row = y_near[0]
 
@@ -301,8 +349,10 @@
         return 0
 
     lax.fori_loop(0, NFAR, choose_j, 0)
+    for s in range(NREM):
+        b = wanted(near_row, s)
+        sel_j[5, s : s + 1, :] = cent_j[lax.shift_right_logical(owner_of(b), 1), 4, pl.ds(within(b), 1), :]
     yj_copy = go(remote(sel_j, got_j, ysend.at[1], yrecv.at[1], y_near))
-    x_copies[3].wait_recv()
     for copy in relays:
         copy.wait_recv()
 
@@ -316,11 +366,11 @@
     lax.fori_loop(0, NFAR, choose_i, 0)
     yi_copy = go(remote(sel_i, got_i, ysend.at[0], yrecv.at[0], y_far))
 
-    for copy in dens_copies:
-        copy.wait_recv()
+    lax.fori_loop(0, 2, step_c, 0)
+    yj_copy.wait_recv()
     near_slot(0)
-
-    yj_copy.wait_recv()
+    lax.fori_loop(2, NREM, step_c, 0)
+
     yi_copy.wait_recv()
 
     def take(s, _):
@@ -352,29 +402,35 @@
             ids = jnp.where(at_lane == s, values(s), ids)
         return ids.astype(F32)
 
-    for ref, first in ((rows_all.at[0], 16), (cols_all.at[7], 32)):
+    for ref, first in ((rows_all.at[0], 16), (cols_far, 32)):
         ref[16:, :] = jnp.zeros((8, BLK), F32)
         ref[16:17, :] = ids_of(lambda s, first=first: stage[first + s], NFAR)
 
-    def far(s, _):
-        one = pl.ds(s, 1)
-        put_rows(fa, left_rows(*(far_i[d, one, :] for d in range(4))))
-        put_rows(fb, right_rows(*(far_j[d, one, :] for d in range(4))))
-        at = jnp.transpose(fa[...]).astype(BF16)
-        bt = fb[...].astype(BF16)
-        for h in range(2):
-            span = slice(h * 256, (h + 1) * 256)
-            tile[:, span] = lax.rsqrt(jnp.dot(at, bt[:, span], preferred_element_type=F32))
-        to_rows, to_cols = apply(turn(far_i[4, one, :]), far_j[4, one, :])
-        used, mirror = masks(stage[16 + s], stage[32 + s], s, fcount[0])
-        rows_all[0, one, :] = jnp.where(used, to_rows, 0.0)
-        cols_all[7, one, :] = jnp.where(mirror, to_cols, 0.0)
-        return 0
-
-    lax.fori_loop(0, NFAR, far, 0)
+    def far(i, _):
+        for n in range(2):
+            s = 2 * i + n
+            one = pl.ds(s, 1)
+            put_rows(fa.at[n], left_rows(*(far_i[d, one, :] for d in range(4))) + list(split3(far_i[4, one, :])))
+            put_rows(fb.at[n], right_rows(*(far_j[d, one, :] for d in range(4))))
+            at = jnp.transpose(fa[n]).astype(BF16)
+            bt = fb[n].astype(BF16)
+            halves = [
+                lax.rsqrt(jnp.dot(at, bt[:, h * 256 : (h + 1) * 256], preferred_element_type=F32)) for h in range(2)
+            ]
+            to_rows, to_cols = apply(halves, spread(at, 30), far_j[4, one, :])
+            used, mirror = masks(stage[16 + s], stage[32 + s], s, fcount[0])
+            rows_all[0, one, :] = jnp.where(used, to_rows, 0.0)
+            cols_far[one, :] = jnp.where(mirror, to_cols, 0.0)
+        return 0
+
+    lax.fori_loop(0, NFAR // 2, far, 0)
     m_copy = go(remote(rows_all.at[0], rows_all.at[1], msend.at[0], mrecv.at[0], y_far))
+    total = scatter(cols_far[16:17, 0:24].astype(jnp.int32), 0, 128, cols_far[...])
+    for g in range(8):
+        side[g] = total[g * BPD : (g + 1) * BPD, :]
     f_copies = [
-        go(remote(cols_all.at[7], cols_all.at[i], fsend.at[i], frecv.at[i], p)) for i, p in enumerate(row_peers)
+        go(remote(side.at[lax.rem(r + 1 + i, N_ROW)], side_got.at[i], fsend.at[i], frecv.at[i], p))
+        for i, p in enumerate(row_peers)
     ]
 
     near_slot(1)
@@ -395,9 +451,10 @@
     c_copies = [
         go(remote(near_all.at[7], near_all.at[i], csend.at[i], crecv.at[i], p)) for i, p in enumerate(row_peers)
     ]
-    for copy in f_copies:
-        copy.wait_recv()
-    acc = half[xc] + gathered(cols_all, r * BPD, BPD, 16)
+    acc = half[xc] + side[r]
+    for i, copy in enumerate(f_copies):
+        copy.wait_recv()
+        acc = acc + side_got[i]
     for i, copy in enumerate(p_copies):
         copy.wait_recv()
         acc = acc + parts[i]
@@ -410,8 +467,10 @@
         copy.wait_send()
 
     def sent(s, _):
-        for i in range(1, N_ROW):
-            near_copy(i, s).wait_send()
+        for way in range(2):
+            a_copy(way, s).wait_send()
+            b_copy(way, s).wait_send()
+        n_copy(s).wait_send()
         return 0
 
     lax.fori_loop(0, NREM, sent, 0)
@@ -435,15 +494,17 @@
             vmem(4, 5, BPD, BLK),
             vmem(BPD, BLK),
             vmem(5, NFAR, BLK),
+            vmem(6, NFAR, BLK),
+            vmem(5, NFAR, BLK),
+            vmem(6, NFAR, BLK),
             vmem(5, NFAR, BLK),
             vmem(5, NFAR, BLK),
-            vmem(5, NFAR, BLK),
-            vmem(5, NFAR, BLK),
-            vmem(5, NFAR, BLK),
-            vmem(N_ROW - 1, NREM, 4, 4, BLK),
-            vmem(N_ROW - 1, 8, BLK),
-            vmem(NREM, N_ROW, 4, 4, BLK),
-            vmem(N_ROW, 8, BLK),
+            vmem(NREM, 2, 4, 4, BLK),
+            vmem(NREM, 2, 4, 4, BLK),
+            vmem(NREM, 2, 2, 4, 4, BLK),
+            vmem(NREM, 2, 2, 4, 4, BLK),
+            vmem(NREM, 4, 4, BLK),
+            vmem(NREM, 4, 4, BLK),
             vmem(128, BLK),
             vmem(128, BLK),
             vmem(NNEAR, BLK, 128, dtype=BF16),
@@ -453,16 +514,18 @@
             vmem(4, 128, BLK, dtype=BF16),
             vmem(BLK, BLK),
             vmem(4, 4, BLK),
-            vmem(32, BLK),
-            vmem(32, BLK),
+            vmem(2, 48, BLK),
+            vmem(2, 48, BLK),
             vmem(2, 24, BLK),
-            vmem(8, 24, BLK),
+            vmem(24, BLK),
             vmem(9, 8, BLK),
             vmem(8, BPD, BLK),
             vmem(7, BPD, BLK),
+            vmem(8, BPD, BLK),
+            vmem(7, BPD, BLK),
             dma((BPD + 1,)),
-            dma((8,)), dma((8,)), dma((7,)), dma((7,)), dma((3,)), dma((3,)),
-            dma((7, NREM)), dma((7, NREM)), dma((7,)), dma((7,)), dma((2,)), dma((2,)),
+            dma((8,)), dma((8,)), dma((8,)), dma((8,)), dma((4,)), dma((4,)),
+            dma((2, NREM)), dma((2, NREM)), dma((2, NREM)), dma((2, NREM)), dma((NREM,)), dma((NREM,)), dma((2,)), dma((2,)),
             dma((1,)), dma((1,)), dma((7,)), dma((7,)), dma((7,)), dma((7,)), dma((7,)), dma((7,)),
         ],
         compiler_params=pltpu.CompilerParams(collective_id=0, has_side_effects=True, vmem_limit_bytes=64 << 20),

time: 65.9 us -> 60.5 us (0.918)
  Pallas kernels: 62.9 us -> 57.5 us
    pallas_call x1, Pallas kernels: 62.9 us -> 57.5 us  [body(): pl.pallas_call(potential_kernel, out_shape=jax.ShapeDtypeStruct((BPD * 4,...]
where the time goes in v3:
time: 60.5 us; the launch traced here: 60.2 us
  Pallas kernels  57.5 us (95%)
  local copies, waits for them, and re-layouts  1.38 us (2%)
  between operations  1.31 us (2%)
    pallas_call x1, Pallas kernels, body(): pl.pallas_call(potential_kernel, out_shape=jax.ShapeDtypeStruct((BPD * 4,...  57.5 us
    unnamed x1, local copies, waits for them, and re-layouts  1.38 us

profile of v3, /device:TPU:0, one launch (start us, length us, event | category | flops | bytes accessed | tf_op | source)
XLA Modules:
  0.0 60.2 jit_solution(10864454769539225475)
XLA Ops:
  1.3 57.5 %shard_map.64 = f32[64,128]{1,0:T(8,128)} custom-call(f32[4,4,8192]{2,1,0:T(4,128)} %pts_hbm.1, f32[64,128]{1,0:T(8,128)} %bitcast.5, s32[2,6]{1,0:T(2,128)} %bitcast.6, s32[2,16]{1,0:T(2,128)} %bitcast.7, s32[1]{0:T(128)S(6)} %copy.8.ncount, s32[1]{0:T(128)S(6)} %copy.9.fcount), custom_call_target="tpu_custom_call" | custom-call | tf_op jit(solution)/shard_map/pallas_call | solution.py:483
  58.8 1.4 %copy.10 = f32[8192]{0:T(1024)} copy(f32[8192]{0:T(1024)} %bitcast.4) | data formatting | bytes 65536

commit v4 on v3

--- a/solution.py
+++ b/solution.py
@@ -90,7 +90,7 @@
 def potential_kernel(
     pts_hbm, dens_hbm, npairs, fpairs, ncount, fcount,
     out,
-    lists, stage, blocks, dens, cent_i, cent_j, own_dens, sel_i, sel_j, got_i, got_j, far_i, far_j,
+    lists, stage, blocks, dens, cent_i, cent_j, own_dens, sel_j, got_j, sel_d, got_d, far_i, far_j,
     apack, agot, bpack, bgot, cpack, cgot,
     abuf, bbuf, left, turned, mids, lhs, rhs, tile, pj, fa, fb,
     rows_all, cols_far, near_all, half, parts, side, side_got,
@@ -134,7 +134,7 @@
     bbuf[120:, :] = jnp.zeros((8, BLK), F32)
     fa[:, 32:, :] = jnp.zeros((2, 16, BLK), F32)
     fb[:, 30:, :] = jnp.zeros((2, 18, BLK), F32)
-    sel_j[5] = jnp.zeros((NFAR, BLK), F32)
+    sel_d[...] = jnp.zeros((8, BLK), F32)
     for copy in loads:
         copy.wait()
 
@@ -143,15 +143,15 @@
         w = p[3]
         total = jnp.sum(w, axis=0, keepdims=True)
         for d in range(3):
-            cent_i[xc, d, pl.ds(k, 1), :] = jnp.sum(p[d] * w, axis=0, keepdims=True) / total
-        cent_i[xc, 3, pl.ds(k, 1), :] = total
+            cent_i[c, d, pl.ds(k, 1), :] = jnp.sum(p[d] * w, axis=0, keepdims=True) / total
+        cent_i[c, 3, pl.ds(k, 1), :] = total
         return 0
 
     lax.fori_loop(0, BPD, centroid, 0)
     for q in range(4):
         own_dens[:, q * 128 : (q + 1) * 128] = dens[pl.ds(q, BPD, stride=4), :]
-    cent_i[xc, 4] = own_dens[...]
-    cent_j[z] = cent_i[xc]
+    cent_i[c, 4] = own_dens[...]
+    cent_j[z] = cent_i[c]
 
     pl.semaphore_wait(barrier, len(everyone))
 
@@ -168,7 +168,6 @@
         return copy
 
     list_copies = [go(remote(stage, lists.at[r], lsend.at[i], lrecv.at[i], p)) for i, p in enumerate(row_peers)]
-    list_copies.append(go(remote(stage, lists.at[N_ROW], lsend.at[7], lrecv.at[7], y_far)))
     def ring(buf, index, up, down, send, recv):
         here, above, below = index(0), index(1), index(3)
         first = [
@@ -187,17 +186,22 @@
 
         return second
 
-    def x_index(i):
-        return lax.rem(x + i, 4) * 2 + core
-
-    x_second = ring(cent_i, x_index, x_up, x_down, xsend, xrecv)
+    def x_index(i, side):
+        return (yhi if side == 0 else 1 - yhi) * 8 + lax.rem(x + i, 4) * 2 + core
+
+    def x_ring(side):
+        return ring(cent_i, lambda i: x_index(i, side), x_up, x_down, xsend.at[side], xrecv.at[side])
+
+    relays = []
+
+    def to_core(side, i):
+        part = cent_i.at[x_index(i, side)]
+        relays.append(go(remote(part, part, xsend.at[side, 4 + i], xrecv.at[side, 4 + i], core_peer)))
+
+    yi_copy = go(remote(cent_i.at[c], cent_i.at[c], ysend.at[0], yrecv.at[0], y_far))
+    x_second = x_ring(0)
     z_second = ring(cent_j, lambda i: zs[i], z_up, z_down, zsend, zrecv)
-
-    def to_core(i, sem):
-        part = cent_i.at[x_index(i)]
-        return go(remote(part, part, xsend.at[sem], xrecv.at[sem], core_peer))
-
-    relays = [to_core(0, 4)]
+    to_core(0, 0)
 
     lane = lax.broadcasted_iota(jnp.int32, (BLK, 128), 1) % 4
     ri = lax.broadcasted_iota(jnp.int32, (128, 128), 0)
@@ -315,7 +319,7 @@
         owner = owner_of(b)
         pj[...] = jnp.where(item_mask(owner & 1, ylo), assembled(ylo, s), cgot[s])
         here = cent_j[lax.shift_right_logical(owner, 1), 4, pl.ds(within(b), 1), :]
-        d = jnp.where(same_rows(owner & 1, ylo), here, got_j[5, pl.ds(s, 1), :])
+        d = jnp.where(same_rows(owner & 1, ylo), here, got_d[pl.ds(s, 1), :])
         near_right(s + 1, pj, d)
 
     for m in range(7, 9):
@@ -327,19 +331,25 @@
     lax.fori_loop(0, NREM, step_a, 0)
     x_half = x_second()
     z_half = z_second()
-    relays += [to_core(3, 5), to_core(1, 6)]
+    to_core(0, 3)
+    to_core(0, 1)
+    lax.fori_loop(0, NREM, step_b, 0)
+    yi_copy.wait_recv()
+    x_second = x_ring(1)
+    to_core(1, 0)
 
     k0 = within(stage[0])
     pj[...] = blocks[k0]
     near_right(0, pj, own_dens[pl.ds(k0, 1), :])
 
-    lax.fori_loop(0, NREM, step_b, 0)
-    for copy in x_half:
-        copy.wait_recv()
-    relays.append(to_core(2, 7))
     for copy in z_half:
         copy.wait_recv()
     near_row = y_near[0]
+    for s in range(NREM):
+        b = wanted(near_row, s)
+        sel_d[s : s + 1, :] = cent_j[lax.shift_right_logical(owner_of(b), 1), 4, pl.ds(within(b), 1), :]
+    yd_copy = go(remote(sel_d, got_d, ysend.at[2], yrecv.at[2], y_near))
+    lax.fori_loop(0, 1, step_c, 0)
 
     def choose_j(s, _):
         b = lists[near_row, 32 + s]
@@ -349,37 +359,31 @@
         return 0
 
     lax.fori_loop(0, NFAR, choose_j, 0)
-    for s in range(NREM):
-        b = wanted(near_row, s)
-        sel_j[5, s : s + 1, :] = cent_j[lax.shift_right_logical(owner_of(b), 1), 4, pl.ds(within(b), 1), :]
     yj_copy = go(remote(sel_j, got_j, ysend.at[1], yrecv.at[1], y_near))
+    for copy in x_half:
+        copy.wait_recv()
+    to_core(0, 2)
+    x_half = x_second()
+    to_core(1, 3)
+    to_core(1, 1)
+    lax.fori_loop(1, 2, step_c, 0)
+    yd_copy.wait_recv()
+    near_slot(0)
+    for copy in x_half:
+        copy.wait_recv()
+    to_core(1, 2)
+    lax.fori_loop(2, NREM, step_c, 0)
+    near_slot(1)
+
+    yj_copy.wait_recv()
     for copy in relays:
         copy.wait_recv()
-
-    def choose_i(s, _):
-        a = lists[N_ROW, 16 + s]
-        g, k = owner_of(a) & 7, within(a)
-        for f in range(5):
-            sel_i[f, pl.ds(s, 1), :] = cent_i[g, f, pl.ds(k, 1), :]
-        return 0
-
-    lax.fori_loop(0, NFAR, choose_i, 0)
-    yi_copy = go(remote(sel_i, got_i, ysend.at[0], yrecv.at[0], y_far))
-
-    lax.fori_loop(0, 2, step_c, 0)
-    yj_copy.wait_recv()
-    near_slot(0)
-    lax.fori_loop(2, NREM, step_c, 0)
-
-    yi_copy.wait_recv()
 
     def take(s, _):
         a, b = stage[16 + s], stage[32 + s]
-        owner, k = owner_of(a), within(a)
-        here = same_rows(lax.shift_right_logical(owner, 3), yhi)
         one = pl.ds(s, 1)
         for f in range(5):
-            far_i[f, one, :] = jnp.where(here, cent_i[owner & 7, f, pl.ds(k, 1), :], got_i[f, one, :])
+            far_i[f, one, :] = cent_i[owner_of(a), f, pl.ds(within(a), 1), :]
         owner, k = owner_of(b), within(b)
         here = same_rows(owner & 1, ylo)
         for f in range(5):
@@ -433,7 +437,7 @@
         for i, p in enumerate(row_peers)
     ]
 
-    near_slot(1)
+    near_slot(2)
 
     m_copy.wait_recv()
     total = gathered(rows_all, yhi * 128, 128, 16)
@@ -444,7 +448,7 @@
         to = lax.rem(xc + 1 + i, 8)
         p_copies.append(go(remote(half.at[to], parts.at[i], psend.at[i], precv.at[i], p)))
 
-    lax.fori_loop(2, NREM, lambda s, v: (near_slot(s), v)[1], 0)
+    lax.fori_loop(3, NREM, lambda s, v: (near_slot(s), v)[1], 0)
 
     near_all[8, 6:7, :] = ids_of(lambda s: within(stage[s]) + r * BPD, NNEAR)
     near_all[7, 6:7, :] = ids_of(lambda s: stage[NNEAR + s], NNEAR)
@@ -486,17 +490,17 @@
         in_specs=[hbm, hbm, smem, smem, smem, smem],
         out_specs=pl.BlockSpec(memory_space=pltpu.VMEM),
         scratch_shapes=[
-            pltpu.SMEM((N_ROW + 1, LIST), jnp.int32),
+            pltpu.SMEM((N_ROW, LIST), jnp.int32),
             pltpu.SMEM((LIST,), jnp.int32),
             vmem(BPD, 4, 4, BLK),
             vmem(BPD * 4, 128),
-            vmem(8, 5, BPD, BLK),
+            vmem(N_COL, 5, BPD, BLK),
             vmem(4, 5, BPD, BLK),
             vmem(BPD, BLK),
             vmem(5, NFAR, BLK),
-            vmem(6, NFAR, BLK),
             vmem(5, NFAR, BLK),
-            vmem(6, NFAR, BLK),
+            vmem(8, BLK),
+            vmem(8, BLK),
             vmem(5, NFAR, BLK),
             vmem(5, NFAR, BLK),
             vmem(NREM, 2, 4, 4, BLK),
@@ -524,8 +528,8 @@
             vmem(8, BPD, BLK),
             vmem(7, BPD, BLK),
             dma((BPD + 1,)),
-            dma((8,)), dma((8,)), dma((8,)), dma((8,)), dma((4,)), dma((4,)),
-            dma((2, NREM)), dma((2, NREM)), dma((2, NREM)), dma((2, NREM)), dma((NREM,)), dma((NREM,)), dma((2,)), dma((2,)),
+            dma((7,)), dma((7,)), dma((2, 8)), dma((2, 8)), dma((4,)), dma((4,)),
+            dma((2, NREM)), dma((2, NREM)), dma((2, NREM)), dma((2, NREM)), dma((NREM,)), dma((NREM,)), dma((3,)), dma((3,)),
             dma((1,)), dma((1,)), dma((7,)), dma((7,)), dma((7,)), dma((7,)), dma((7,)), dma((7,)),
         ],
         compiler_params=pltpu.CompilerParams(collective_id=0, has_side_effects=True, vmem_limit_bytes=64 << 20),

time: 60.5 us -> 56.2 us (0.929)
  Pallas kernels: 57.5 us -> 53.3 us
    pallas_call x1, Pallas kernels: 57.5 us -> 53.3 us  [body(): pl.pallas_call(potential_kernel, out_shape=jax.ShapeDtypeStruct((BPD * 4,...]
where the time goes in v4:
time: 56.2 us; the launch traced here: 55.9 us
  Pallas kernels  53.3 us (95%)
  local copies, waits for them, and re-layouts  1.38 us (2%)
  between operations  1.31 us (2%)
    pallas_call x1, Pallas kernels, body(): pl.pallas_call(potential_kernel, out_shape=jax.ShapeDtypeStruct((BPD * 4,...  53.3 us
    unnamed x1, local copies, waits for them, and re-layouts  1.38 us

profile of v4, /device:TPU:0, one launch (start us, length us, event | category | flops | bytes accessed | tf_op | source)
XLA Modules:
  0.0 55.9 jit_solution(8335213321408272833)
XLA Ops:
  1.3 53.3 %shard_map.64 = f32[64,128]{1,0:T(8,128)} custom-call(f32[4,4,8192]{2,1,0:T(4,128)} %pts_hbm.1, f32[64,128]{1,0:T(8,128)} %bitcast.5, s32[2,6]{1,0:T(2,128)} %bitcast.6, s32[2,16]{1,0:T(2,128)} %bitcast.7, s32[1]{0:T(128)S(6)} %copy.8.ncount, s32[1]{0:T(128)S(6)} %copy.9.fcount), custom_call_target="tpu_custom_call" | custom-call | tf_op jit(solution)/shard_map/pallas_call | solution.py:487
  54.6 1.4 %copy.10 = f32[8192]{0:T(1024)} copy(f32[8192]{0:T(1024)} %bitcast.4) | data formatting | bytes 65536

commit v5 on v4

--- a/solution.py
+++ b/solution.py
@@ -88,11 +88,11 @@
 
 
 def potential_kernel(
-    pts_hbm, dens_hbm, npairs, fpairs, ncount, fcount,
+    pts_hbm, dens_hbm, npairs, fpairs, ncount_hbm, fcount_hbm,
     out,
-    lists, stage, blocks, dens, cent_i, cent_j, own_dens, sel_j, got_j, sel_d, got_d, far_i, far_j,
+    ncount, fcount, lists, stage, blocks, dens, cent_i, cent_j, own_dens, sel_j, got_j, sel_d, got_d, far_i, far_j,
     apack, agot, bpack, bgot, cpack, cgot,
-    abuf, bbuf, left, turned, mids, lhs, rhs, tile, pj, fa, fb,
+    abuf, bbuf, turned, mids, lhs, rhs, tile, pj, fa, fb, fd, fat, fbt, fdt,
     rows_all, cols_far, near_all, half, parts, side, side_got,
     load, lsend, lrecv, xsend, xrecv, zsend, zrecv, asend, arecv, bsend, brecv, nsend, nrecv, ysend, yrecv,
     msend, mrecv, fsend, frecv, csend, crecv, psend, precv,
@@ -120,6 +120,8 @@
         pltpu.make_async_copy(pts_hbm.at[:, :, pl.ds(k * BLK, BLK)], blocks.at[k], load.at[k]) for k in range(BPD)
     ]
     loads.append(pltpu.make_async_copy(dens_hbm, dens, load.at[BPD]))
+    loads.append(pltpu.make_async_copy(ncount_hbm, ncount, load.at[BPD + 1]))
+    loads.append(pltpu.make_async_copy(fcount_hbm, fcount, load.at[BPD + 2]))
     for copy in loads:
         copy.start()
 
@@ -132,8 +134,9 @@
         stage[32 + s] = fpairs[1, s]
     abuf[120:, :] = jnp.zeros((8, BLK), F32)
     bbuf[120:, :] = jnp.zeros((8, BLK), F32)
-    fa[:, 32:, :] = jnp.zeros((2, 16, BLK), F32)
-    fb[:, 30:, :] = jnp.zeros((2, 18, BLK), F32)
+    fa[240:, :] = jnp.zeros((16, BLK), F32)
+    fb[240:, :] = jnp.zeros((16, BLK), F32)
+    fd[24:, :] = jnp.zeros((8, BLK), F32)
     sel_d[...] = jnp.zeros((8, BLK), F32)
     for copy in loads:
         copy.wait()
@@ -207,11 +210,9 @@
     ri = lax.broadcasted_iota(jnp.int32, (128, 128), 0)
     ci = lax.broadcasted_iota(jnp.int32, (128, 128), 1)
 
-    def spread(turned_rows, first):
-        n = turned_rows.shape[1]
-        k = lax.broadcasted_iota(jnp.int32, (n, 128), 0)
-        pick = jnp.where((k >= first) & (k < first + 3), 1.0, 0.0).astype(BF16)
-        return jnp.dot(turned_rows, pick, preferred_element_type=F32)
+    def spread(turned_rows, chosen):
+        k = lax.broadcasted_iota(jnp.int32, (turned_rows.shape[1], 128), 0)
+        return jnp.dot(turned_rows, jnp.where(chosen(k), 1.0, 0.0).astype(BF16), preferred_element_type=F32)
 
     def apply(halves, column, dj):
         part = None
@@ -236,8 +237,9 @@
         put_rows(abuf, left_rows(*(p[d] - mid[d] for d in range(3)), p[3]))
         put_rows(abuf.at[120:123], split3(own_dens[pl.ds(k, 1), :]))
         at = jnp.transpose(abuf[...]).astype(BF16)
-        left[s] = at
-        turned[s] = spread(at, 120)
+        for u in range(4):
+            lhs[s, u] = jnp.where(lane == u, at, jnp.zeros_like(at))
+        turned[s] = spread(at, lambda k: (k >= 120) & (k < 123))
         for d in range(3):
             mids[s, d : d + 1, :] = jnp.full((1, BLK), mid[d], F32)
         return 0
@@ -249,15 +251,12 @@
         for t in range(1, 4):
             shift = jnp.where((ri // 4 == ci // 4) & ((ri % 4 + t) % 4 == ci % 4), 1.0, 0.0).astype(BF16)
             rhs[t] = jnp.dot(shift, bt, preferred_element_type=F32).astype(BF16)
-        at = left[s]
-        for u in range(4):
-            lhs[u] = jnp.where(lane == u, at, jnp.zeros_like(at))
         for t in range(4):
             for h in range(2):
                 span = slice(h * 256, (h + 1) * 256)
                 acc = None
                 for u in range(4):
-                    v = lax.rsqrt(jnp.dot(lhs[u], rhs[t][:, span], preferred_element_type=F32))
+                    v = lax.rsqrt(jnp.dot(lhs[s, u], rhs[t][:, span], preferred_element_type=F32))
                     acc = v if acc is None else acc + v
                 if t == 0:
                     tile[:, span] = acc
@@ -324,7 +323,7 @@
 
     for m in range(7, 9):
         near_all[m] = jnp.zeros((8, BLK), F32)
-    lax.fori_loop(0, NNEAR, near_left, 0)
+    lax.fori_loop(0, 2, near_left, 0)
 
     for copy in list_copies:
         copy.wait_recv()
@@ -333,14 +332,19 @@
     z_half = z_second()
     to_core(0, 3)
     to_core(0, 1)
+
+    k0 = within(stage[0])
+    pj[...] = blocks[k0]
+    near_right(0, pj, own_dens[pl.ds(k0, 1), :])
+
     lax.fori_loop(0, NREM, step_b, 0)
     yi_copy.wait_recv()
     x_second = x_ring(1)
     to_core(1, 0)
-
-    k0 = within(stage[0])
-    pj[...] = blocks[k0]
-    near_right(0, pj, own_dens[pl.ds(k0, 1), :])
+    lax.fori_loop(2, NNEAR, near_left, 0)
+    for copy in x_half:
+        copy.wait_recv()
+    to_core(0, 2)
 
     for copy in z_half:
         copy.wait_recv()
@@ -349,7 +353,6 @@
         b = wanted(near_row, s)
         sel_d[s : s + 1, :] = cent_j[lax.shift_right_logical(owner_of(b), 1), 4, pl.ds(within(b), 1), :]
     yd_copy = go(remote(sel_d, got_d, ysend.at[2], yrecv.at[2], y_near))
-    lax.fori_loop(0, 1, step_c, 0)
 
     def choose_j(s, _):
         b = lists[near_row, 32 + s]
@@ -360,13 +363,10 @@
 
     lax.fori_loop(0, NFAR, choose_j, 0)
     yj_copy = go(remote(sel_j, got_j, ysend.at[1], yrecv.at[1], y_near))
-    for copy in x_half:
-        copy.wait_recv()
-    to_core(0, 2)
+    lax.fori_loop(0, 2, step_c, 0)
     x_half = x_second()
     to_core(1, 3)
     to_core(1, 1)
-    lax.fori_loop(1, 2, step_c, 0)
     yd_copy.wait_recv()
     near_slot(0)
     for copy in x_half:
@@ -410,18 +410,29 @@
         ref[16:, :] = jnp.zeros((8, BLK), F32)
         ref[16:17, :] = ids_of(lambda s, first=first: stage[first + s], NFAR)
 
+    for g in range(2):
+        eight = slice(g * 8, g * 8 + 8)
+        put_rows(fa, left_rows(*(far_i[d, eight, :] for d in range(4))))
+        put_rows(fb, right_rows(*(far_j[d, eight, :] for d in range(4))))
+        put_rows(fd, split3(far_i[4, eight, :]))
+        fat[g] = jnp.transpose(fa[...]).astype(BF16)
+        fbt[g] = fb[...].astype(BF16)
+        fdt[g] = jnp.transpose(fd[...]).astype(BF16)
+    far_lane = lax.broadcasted_iota(jnp.int32, (BLK, 256), 1) % 8
+
     def far(i, _):
         for n in range(2):
             s = 2 * i + n
+            g, e = s // 8, lax.rem(s, 8)
             one = pl.ds(s, 1)
-            put_rows(fa.at[n], left_rows(*(far_i[d, one, :] for d in range(4))) + list(split3(far_i[4, one, :])))
-            put_rows(fb.at[n], right_rows(*(far_j[d, one, :] for d in range(4))))
-            at = jnp.transpose(fa[n]).astype(BF16)
-            bt = fb[n].astype(BF16)
+            at = fat[g]
+            at = jnp.where(far_lane == e, at, jnp.zeros_like(at))
             halves = [
-                lax.rsqrt(jnp.dot(at, bt[:, h * 256 : (h + 1) * 256], preferred_element_type=F32)) for h in range(2)
+                lax.rsqrt(jnp.dot(at, fbt[g, :, h * 256 : (h + 1) * 256], preferred_element_type=F32))
+                for h in range(2)
             ]
-            to_rows, to_cols = apply(halves, spread(at, 30), far_j[4, one, :])
+            column = spread(fdt[g], lambda k, e=e: (k % 8 == e) & (k < 24))
+            to_rows, to_cols = apply(halves, column, far_j[4, one, :])
             used, mirror = masks(stage[16 + s], stage[32 + s], s, fcount[0])
             rows_all[0, one, :] = jnp.where(used, to_rows, 0.0)
             cols_far[one, :] = jnp.where(mirror, to_cols, 0.0)
@@ -437,7 +448,7 @@
         for i, p in enumerate(row_peers)
     ]
 
-    near_slot(2)
+    lax.fori_loop(2, 4, lambda s, v: (near_slot(s), v)[1], 0)
 
     m_copy.wait_recv()
     total = gathered(rows_all, yhi * 128, 128, 16)
@@ -448,7 +459,7 @@
         to = lax.rem(xc + 1 + i, 8)
         p_copies.append(go(remote(half.at[to], parts.at[i], psend.at[i], precv.at[i], p)))
 
-    lax.fori_loop(3, NREM, lambda s, v: (near_slot(s), v)[1], 0)
+    near_slot(4)
 
     near_all[8, 6:7, :] = ids_of(lambda s: within(stage[s]) + r * BPD, NNEAR)
     near_all[7, 6:7, :] = ids_of(lambda s: stage[NNEAR + s], NNEAR)
@@ -487,9 +498,11 @@
     out = pl.pallas_call(
         potential_kernel,
         out_shape=jax.ShapeDtypeStruct((BPD * 4, 128), F32),
-        in_specs=[hbm, hbm, smem, smem, smem, smem],
+        in_specs=[hbm, hbm, smem, smem, hbm, hbm],
         out_specs=pl.BlockSpec(memory_space=pltpu.VMEM),
         scratch_shapes=[
+            pltpu.SMEM((1,), jnp.int32),
+            pltpu.SMEM((1,), jnp.int32),
             pltpu.SMEM((N_ROW, LIST), jnp.int32),
             pltpu.SMEM((LIST,), jnp.int32),
             vmem(BPD, 4, 4, BLK),
@@ -511,15 +524,18 @@
             vmem(NREM, 4, 4, BLK),
             vmem(128, BLK),
             vmem(128, BLK),
-            vmem(NNEAR, BLK, 128, dtype=BF16),
             vmem(NNEAR, BLK, 128),
             vmem(NNEAR, 8, BLK),
-            vmem(4, BLK, 128, dtype=BF16),
+            vmem(NNEAR, 4, BLK, 128, dtype=BF16),
             vmem(4, 128, BLK, dtype=BF16),
             vmem(BLK, BLK),
             vmem(4, 4, BLK),
-            vmem(2, 48, BLK),
-            vmem(2, 48, BLK),
+            vmem(256, BLK),
+            vmem(256, BLK),
+            vmem(32, BLK),
+            vmem(2, BLK, 256, dtype=BF16),
+            vmem(2, 256, BLK, dtype=BF16),
+            vmem(2, BLK, 32, dtype=BF16),
             vmem(2, 24, BLK),
             vmem(24, BLK),
             vmem(9, 8, BLK),
@@ -527,7 +543,7 @@
             vmem(7, BPD, BLK),
             vmem(8, BPD, BLK),
             vmem(7, BPD, BLK),
-            dma((BPD + 1,)),
+            dma((BPD + 3,)),
             dma((7,)), dma((7,)), dma((2, 8)), dma((2, 8)), dma((4,)), dma((4,)),
             dma((2, NREM)), dma((2, NREM)), dma((2, NREM)), dma((2, NREM)), dma((NREM,)), dma((NREM,)), dma((3,)), dma((3,)),
             dma((1,)), dma((1,)), dma((7,)), dma((7,)), dma((7,)), dma((7,)), dma((7,)), dma((7,)),

time: 56.2 us -> 54 us (0.961)
  Pallas kernels: 53.3 us -> 51 us
    pallas_call x1, Pallas kernels: 53.3 us -> 51 us  [body(): pl.pallas_call(potential_kernel, out_shape=jax.ShapeDtypeStruct((BPD * 4,...]
where the time goes in v5:
time: 54 us; the launch traced here: 53.7 us
  Pallas kernels  51 us (94%)
  local copies, waits for them, and re-layouts  1.38 us (3%)
  between operations  1.31 us (2%)
    pallas_call x1, Pallas kernels, body(): pl.pallas_call(potential_kernel, out_shape=jax.ShapeDtypeStruct((BPD * 4,...  51 us
    unnamed x1, local copies, waits for them, and re-layouts  1.38 us

profile of v5, /device:TPU:0, one launch (start us, length us, event | category | flops | bytes accessed | tf_op | source)
XLA Modules:
  0.0 53.7 jit_solution(1384949149571226039)
XLA Ops:
  1.3 51.0 %shard_map.64 = f32[64,128]{1,0:T(8,128)} custom-call(f32[4,4,8192]{2,1,0:T(4,128)} %pts_hbm.1, f32[64,128]{1,0:T(8,128)} %bitcast.5, s32[2,6]{1,0:T(2,128)} %bitcast.6, s32[2,16]{1,0:T(2,128)} %bitcast.7, s32[1]{0:T(128)S(6)} %copy.8.ncount_hbm, s32[1]{0:T(128)S(6)} %copy.9.fcount_hbm), custom_call_target="tpu_custom_call" | custom-call | tf_op jit(solution)/shard_map/pallas_call | solution.py:498
  52.3 1.4 %copy.10 = f32[8192]{0:T(1024)} copy(f32[8192]{0:T(1024)} %bitcast.4) | data formatting | bytes 65536

commit v6 on v5

--- a/solution.py
+++ b/solution.py
@@ -251,17 +251,16 @@
         for t in range(1, 4):
             shift = jnp.where((ri // 4 == ci // 4) & ((ri % 4 + t) % 4 == ci % 4), 1.0, 0.0).astype(BF16)
             rhs[t] = jnp.dot(shift, bt, preferred_element_type=F32).astype(BF16)
-        for t in range(4):
-            for h in range(2):
-                span = slice(h * 256, (h + 1) * 256)
+        for h in range(2):
+            span = slice(h * 256, (h + 1) * 256)
+            for i in range(2):
+                rows = slice(i * 256, (i + 1) * 256)
                 acc = None
-                for u in range(4):
-                    v = lax.rsqrt(jnp.dot(lhs[s, u], rhs[t][:, span], preferred_element_type=F32))
-                    acc = v if acc is None else acc + v
-                if t == 0:
-                    tile[:, span] = acc
-                else:
-                    tile[:, span] += acc
+                for t in range(4):
+                    for u in range(4):
+                        v = lax.rsqrt(jnp.dot(lhs[s, u, rows, :], rhs[t][:, span], preferred_element_type=F32))
+                        acc = v if acc is None else acc + v
+                tile[rows, span] = acc
         to_rows, to_cols = apply([tile.at[:, 0:256], tile.at[:, 256:512]], turned[s], dj)
         used, mirror = masks(stage[s], stage[NNEAR + s], s, ncount[0])
         near_all[8, pl.ds(s, 1), :] = jnp.where(used, to_rows, 0.0)

time: 54 us -> 54 us (level)
  no operation moved by 1% of the time
where the time goes in v6:
time: 54 us; the launch traced here: 53.7 us
  Pallas kernels  51 us (94%)
  local copies, waits for them, and re-layouts  1.38 us (3%)
  between operations  1.31 us (2%)
    pallas_call x1, Pallas kernels, body(): pl.pallas_call(potential_kernel, out_shape=jax.ShapeDtypeStruct((BPD * 4,...  51 us
    unnamed x1, local copies, waits for them, and re-layouts  1.38 us

profile of v6, /device:TPU:0, one launch (start us, length us, event | category | flops | bytes accessed | tf_op | source)
XLA Modules:
  0.0 53.7 jit_solution(1012270588183503814)
XLA Ops:
  1.3 51.0 %shard_map.64 = f32[64,128]{1,0:T(8,128)} custom-call(f32[4,4,8192]{2,1,0:T(4,128)} %pts_hbm.1, f32[64,128]{1,0:T(8,128)} %bitcast.5, s32[2,6]{1,0:T(2,128)} %bitcast.6, s32[2,16]{1,0:T(2,128)} %bitcast.7, s32[1]{0:T(128)S(6)} %copy.8.ncount_hbm, s32[1]{0:T(128)S(6)} %copy.9.fcount_hbm), custom_call_target="tpu_custom_call" | custom-call | tf_op jit(solution)/shard_map/pallas_call | solution.py:497
  52.3 1.4 %copy.10 = f32[8192]{0:T(1024)} copy(f32[8192]{0:T(1024)} %bitcast.4) | data formatting | bytes 65536

commit v7 on v6

--- a/solution.py
+++ b/solution.py
@@ -439,14 +439,6 @@
 
     lax.fori_loop(0, NFAR // 2, far, 0)
     m_copy = go(remote(rows_all.at[0], rows_all.at[1], msend.at[0], mrecv.at[0], y_far))
-    total = scatter(cols_far[16:17, 0:24].astype(jnp.int32), 0, 128, cols_far[...])
-    for g in range(8):
-        side[g] = total[g * BPD : (g + 1) * BPD, :]
-    f_copies = [
-        go(remote(side.at[lax.rem(r + 1 + i, N_ROW)], side_got.at[i], fsend.at[i], frecv.at[i], p))
-        for i, p in enumerate(row_peers)
-    ]
-
     lax.fori_loop(2, 4, lambda s, v: (near_slot(s), v)[1], 0)
 
     m_copy.wait_recv()
@@ -457,6 +449,14 @@
     for i, p in enumerate(xc_peers):
         to = lax.rem(xc + 1 + i, 8)
         p_copies.append(go(remote(half.at[to], parts.at[i], psend.at[i], precv.at[i], p)))
+
+    total = scatter(cols_far[16:17, 0:24].astype(jnp.int32), 0, 128, cols_far[...])
+    for g in range(8):
+        side[g] = total[g * BPD : (g + 1) * BPD, :]
+    f_copies = [
+        go(remote(side.at[lax.rem(r + 1 + i, N_ROW)], side_got.at[i], fsend.at[i], frecv.at[i], p))
+        for i, p in enumerate(row_peers)
+    ]
 
     near_slot(4)
 

time: 54 us -> 54 us (level)
  no operation moved by 1% of the time
where the time goes in v7:
time: 54 us; the launch traced here: 53.7 us
  Pallas kernels  51 us (94%)
  local copies, waits for them, and re-layouts  1.38 us (3%)
  between operations  1.31 us (2%)
    pallas_call x1, Pallas kernels, body(): pl.pallas_call(potential_kernel, out_shape=jax.ShapeDtypeStruct((BPD * 4,...  51 us
    unnamed x1, local copies, waits for them, and re-layouts  1.38 us

profile of v7, /device:TPU:0, one launch (start us, length us, event | category | flops | bytes accessed | tf_op | source)
XLA Modules:
  0.0 53.7 jit_solution(13714596310124811576)
XLA Ops:
  1.3 51.0 %shard_map.64 = f32[64,128]{1,0:T(8,128)} custom-call(f32[4,4,8192]{2,1,0:T(4,128)} %pts_hbm.1, f32[64,128]{1,0:T(8,128)} %bitcast.5, s32[2,6]{1,0:T(2,128)} %bitcast.6, s32[2,16]{1,0:T(2,128)} %bitcast.7, s32[1]{0:T(128)S(6)} %copy.8.ncount_hbm, s32[1]{0:T(128)S(6)} %copy.9.fcount_hbm), custom_call_target="tpu_custom_call" | custom-call | tf_op jit(solution)/shard_map/pallas_call | solution.py:497
  52.3 1.4 %copy.10 = f32[8192]{0:T(1024)} copy(f32[8192]{0:T(1024)} %bitcast.4) | data formatting | bytes 65536
